TPU v7x, 256 devices: a whole 4x4x8 slice. The times are simulated.
256 devices in a mesh: dp: 8 (over z_lo, core), ctx: 32 (over y, z_hi, x).
Axes of the slice: x: 4, y: 4, z: 8 (z_hi: 2, z_lo: 4; z = z_hi * 4 + z_lo), core: 2. Of those that a mesh axis runs over, the one named last changes fastest.
Arguments:
- queries: bfloat16 [8, 6144, 5120], P('dp', 'ctx'), may hold values from -420 to 420
- packed_keys_values: bfloat16 [8, 6144, 2048], P('dp', 'ctx'), may hold values from -5 to 5
- cotangents: bfloat16 [8, 6144, 2, 5120], P('dp', 'ctx'), may hold values from -5 to 5
- send_rows: int32 [8, 32, 32, 7], P('dp', 'ctx'), may hold values from -1 to 191, as said below
- take_slots: int32 [8, 6144], P('dp', 'ctx'), may hold values from 0 to 223, as said below
- segment_ids: int32 [8, 6144], P('dp', 'ctx'), may hold values from 0 to 63, never falling along the last dimension, each value on 1 to 576 neighbouring positions
Outputs:
- attention_out: bfloat16 [8, 6144, 5120], P('dp', 'ctx')
- bias_curvature: float32 [5120], replicated
Inputs may be any that keep to these rules, and one draw needn't show every extreme that they name: send_rows[pack, s, t] lists distinct local rows of device s first and -1 after them; over all t every local row of s is listed once; at most 7 rows from s to t, reached in every pack. take_slots[pack, t * 192 + r] = s * 7 + k names the k-th listed row of send_rows[pack, s, t]; every listed row is named once.
All inputs are finite; a program needn't handle non-finite values.
Results may differ from a plain program's by a relative error of at most 0.0055.
Values may be sent and summed in bfloat16 or wider, within the bound.
A program may use at most 128 MiB of HBM per device.

v0:
```python
import math

import jax
import jax.numpy as jnp
from jax import lax
from jax.sharding import PartitionSpec as P

QUERY_HEADS = 40
KEY_VALUE_HEADS = 8
HEAD_SIZE = 128
GROUP_MOST = 4


def from_behind(block, axis, distance):
    devices = range(lax.axis_size(axis))
    route = [(i - distance, i) for i in devices if i - distance in devices]
    return lax.ppermute(block, axis, route)


def head_forward(query_rows, key_rows, value_rows, allowed):
    score_scale = 1.0 / math.sqrt(query_rows.shape[-1])
    scores = jnp.dot(query_rows, key_rows.T, preferred_element_type=jnp.float32) * score_scale
    masked = jnp.where(allowed, scores, -1e30)
    row_top = jnp.max(masked, axis=1, keepdims=True)
    weights = jnp.where(allowed, jnp.exp(masked - row_top), 0.0)
    probabilities = weights / jnp.sum(weights, axis=1, keepdims=True)
    blended_rows = jnp.dot(
        probabilities.astype(jnp.bfloat16), value_rows, preferred_element_type=jnp.float32
    )
    return (blended_rows, probabilities)


def head_backward(upstream_rows, probabilities, blended_rows, key_rows, value_rows, group_width):
    score_scale = 1.0 / math.sqrt(key_rows.shape[-1])
    bias_grads = []
    for probe_index in range(2):
        upstream = upstream_rows[probe_index]
        row_delta = jnp.sum(upstream.astype(jnp.float32) * blended_rows, axis=1, keepdims=True)
        prob_grad = jnp.dot(upstream, value_rows.T, preferred_element_type=jnp.float32)
        score_grad = probabilities * (prob_grad - row_delta)
        column_sums = jnp.sum(score_grad.reshape(group_width, -1, score_grad.shape[1]), axis=1)
        bias_grads.append(
            jnp.dot(column_sums, key_rows.astype(jnp.float32), precision=lax.Precision.HIGHEST)
            * score_scale
        )
    return jnp.stack(bias_grads)


def per_device(queries, packed_keys_values, cotangents, send_rows, take_slots, segment_ids):
    row_total = queries.shape[1]
    group_width = QUERY_HEADS // KEY_VALUE_HEADS
    owner_count = lax.axis_size("ctx")
    owner_index = lax.axis_index("ctx")
    picked_rows = jnp.maximum(send_rows[0, 0], 0)
    slot_index = take_slots[0]
    outgoing_queries = queries[0][picked_rows]
    outgoing_pairs = packed_keys_values[0][picked_rows]
    outgoing_upstream = cotangents[0][picked_rows]

    def arrange(received):
        flat_rows = received.reshape((-1,) + received.shape[2:])
        return flat_rows[slot_index]

    arrived_queries, arrived_pairs, arrived_upstream = (
        lax.all_to_all(outgoing_queries, "ctx", split_axis=0, concat_axis=0, tiled=True),
        lax.all_to_all(outgoing_pairs, "ctx", split_axis=0, concat_axis=0, tiled=True),
        lax.all_to_all(outgoing_upstream, "ctx", split_axis=0, concat_axis=0, tiled=True),
    )
    resident_queries = arrange(arrived_queries)
    local_pairs = arrange(arrived_pairs)
    segment_local = segment_ids[0]
    segment_wire = segment_local.astype(jnp.bfloat16)
    pair_blocks = [local_pairs]
    segment_blocks = [segment_wire]
    for distance in range(1, GROUP_MOST):
        far_pairs, far_segments = from_behind((local_pairs, segment_wire), "ctx", distance)
        pair_blocks.insert(0, far_pairs)
        segment_blocks.insert(0, far_segments)
    key_value_pairs = jnp.concatenate(pair_blocks, axis=0)
    key_segments = jnp.concatenate(segment_blocks, axis=0)
    key_total = GROUP_MOST * row_total
    key_index = jnp.arange(key_total, dtype=jnp.int32)
    key_block = key_index // row_total
    relative = key_index - (GROUP_MOST - 1) * row_total
    query_index = jnp.arange(row_total, dtype=jnp.int32)
    present = owner_index + key_block - (GROUP_MOST - 1) >= 0
    same_document = (
        key_segments.astype(jnp.float32)[None, :] == segment_local.astype(jnp.float32)[:, None]
    )
    allowed = present[None, :] & (relative[None, :] <= query_index[:, None]) & same_document
    tiled_mask = jnp.tile(allowed, (group_width, 1))
    query_head_rows = (
        resident_queries.reshape(row_total, KEY_VALUE_HEADS, group_width, HEAD_SIZE)
        .transpose(1, 2, 0, 3)
        .reshape(KEY_VALUE_HEADS, group_width * row_total, HEAD_SIZE)
    )
    key_head_rows = (
        key_value_pairs[:, : KEY_VALUE_HEADS * HEAD_SIZE]
        .reshape(key_total, KEY_VALUE_HEADS, HEAD_SIZE)
        .transpose(1, 0, 2)
    )
    value_head_rows = (
        key_value_pairs[:, KEY_VALUE_HEADS * HEAD_SIZE :]
        .reshape(key_total, KEY_VALUE_HEADS, HEAD_SIZE)
        .transpose(1, 0, 2)
    )
    blended_rows, probabilities = lax.map(
        lambda operands: head_forward(operands[0], operands[1], operands[2], tiled_mask),
        (query_head_rows, key_head_rows, value_head_rows),
    )
    attended_rows = (
        blended_rows.reshape(KEY_VALUE_HEADS, group_width, row_total, HEAD_SIZE)
        .transpose(2, 0, 1, 3)
        .reshape(row_total, QUERY_HEADS * HEAD_SIZE)
        .astype(jnp.bfloat16)
    )
    resident_upstream = arrange(arrived_upstream)
    upstream_head_rows = (
        resident_upstream.reshape(row_total, 2, KEY_VALUE_HEADS, group_width, HEAD_SIZE)
        .transpose(2, 1, 3, 0, 4)
        .reshape(KEY_VALUE_HEADS, 2, group_width * row_total, HEAD_SIZE)
    )
    bias_grads = lax.map(
        lambda operands: head_backward(
            operands[0], operands[1], operands[2], operands[3], operands[4], group_width
        ),
        (upstream_head_rows, probabilities, blended_rows, key_head_rows, value_head_rows),
    )
    probe_terms = bias_grads.transpose(1, 0, 2, 3).reshape(2, QUERY_HEADS * HEAD_SIZE)
    totals = lax.psum(probe_terms, ("dp", "ctx"))
    token_total = 2.0 * row_total * owner_count * lax.axis_size("dp")
    bias_curvature = (totals[0] * totals[0] + totals[1] * totals[1]) / token_total
    return (attended_rows[None], bias_curvature)


def solution(mesh):
    placed = (
        P("dp", "ctx", None),
        P("dp", "ctx", None),
        P("dp", "ctx", None, None),
        P("dp", "ctx", None, None),
        P("dp", "ctx"),
        P("dp", "ctx"),
    )
    return jax.shard_map(
        per_device,
        mesh=mesh,
        in_specs=placed,
        out_specs=(P("dp", "ctx", None), P()),
        check_vma=False,
    )
```

profile of v0, /device:TPU:1, one launch (start us, length us, event | category | flops | bytes accessed | tf_op | source)
XLA Modules:
  0.0 614.3 jit_solution(13019667684755998739)
XLA Ops:
  1.7 3.4 gather_fusion.2
  6.3 14.5 %all-to-all-start.1 = ((bf16[32,7,2048]{2,1,0:T(8,128)(2,1)}), bf16[32,7,2048]{2,1,0:T(8,128)(2,1)S(1)}, u32[]{:S(2)}, u32[]{:S(2)}) async-start(bf16[32,7,2048]{2,1,0:T(8,128)(2,1)} %reshape.254), calls=%async_computation.1 | async-start | bytes 2097152 | tf_op jit(solution)/shard_map/all_to_all | solution.py:66
  20.8 3.3 gather_fusion
  24.1 4.2 reshape.238
  28.4 14.3 %all-to-all-done.1 = bf16[32,7,2048]{2,1,0:T(8,128)(2,1)S(1)} async-done(((bf16[32,7,2048]{2,1,0:T(8,128)(2,1)}), bf16[32,7,2048]{2,1,0:T(8,128)(2,1)S(1)}, u32[]{:S(2)}, u32[]{:S(2)}) %all-to-all-start.1) | async-done | bytes 917536 | tf_op jit(solution)/shard_map/all_to_all | solution.py:66
  43.7 4.4 all-to-all-start
  48.1 18.5 %gather_fusion.4 = bf16[224,2,5120]{2,1,0:T(2,128)(2,1)} fusion(bf16[192,2,5120]{2,1,0:T(2,128)(2,1)} %bitcast.161, s32[1024]{0:T(1024)S(1)} %pad_clamp_fusion.1), kind=kCustom, calls=%fused_computation.4 | custom fusion | bytes 9175936 | tf_op jit(solution)/shard_map/gather | solution.py:58
  66.6 11.4 %all-to-all-done = bf16[32,7,5120]{2,1,0:T(8,128)(2,1)S(1)} async-done(((bf16[32,7,5120]{2,1,0:T(8,128)(2,1)}), bf16[32,7,5120]{2,1,0:T(8,128)(2,1)S(1)}, u32[]{:S(2)}, u32[]{:S(2)}) %all-to-all-start) | async-done | bytes 2293792 | tf_op jit(solution)/shard_map/all_to_all | solution.py:65
  79.5 14.3 %all-to-all-start.2 = ((bf16[32,7,2,5120]{3,2,1,0:T(2,128)(2,1)}), bf16[32,7,2,5120]{3,2,1,0:T(2,128)(2,1)}, u32[]{:S(2)}, u32[]{:S(2)}) async-start(bf16[32,7,2,5120]{3,2,1,0:T(2,128)(2,1)} %bitcast.157), calls=%async_computation.2 | async-start | bytes 9175040 | tf_op jit(solution)/shard_map/all_to_all | solution.py:67
  96.5 4.3 collective-permute-start
  100.9 7.2 %collective-permute-start.3 = (bf16[192]{0:T(256)(128)(2,1)S(1)}, bf16[192]{0:T(256)(128)(2,1)S(1)}, u32[]{:S(2)}, u32[]{:S(2)}) collective-permute-start(bf16[192]{0:T(256)(128)(2,1)S(1)} %convert_reduce_fusion), channel_id=1, source_target_pairs={{0,3},{1,4},{2,5},{3,6},{4,7},{5,8},{6,9},{7,10},{8,11},{9,12},{10... | collective-permute-start | bytes 1160 | tf_op jit(solution)/shard_map/ppermute | solution.py:17
  113.7 5.6 collective-permute-start.1
  119.3 47.7 %collective-permute-done.3 = bf16[192]{0:T(256)(128)(2,1)S(1)} collective-permute-done((bf16[192]{0:T(256)(128)(2,1)S(1)}, bf16[192]{0:T(256)(128)(2,1)S(1)}, u32[]{:S(2)}, u32[]{:S(2)}) %collective-permute-start.3) | collective-permute-done | bytes 416 | tf_op jit(solution)/shard_map/ppermute | solution.py:17
  167.1 18.6 %collective-permute-start.2 = (bf16[192,2048]{1,0:T(8,128)(2,1)S(1)}, bf16[192,2048]{1,0:T(8,128)(2,1)S(1)}, u32[]{:S(2)}, u32[]{:S(2)}) collective-permute-start(bf16[192,2048]{1,0:T(8,128)(2,1)S(1)} %gather_fusion.3), channel_id=1, source_target_pairs={{0,1},{1,2},{2,3},{3,4},{4,5},{5,6},{6,7},{7,8},{8,9},{9,10},{10,1... | collective-permute-start | bytes 2359304 | tf_op jit(solution)/shard_map/ppermute | solution.py:17
  186.1 15.6 %collective-permute-done.2 = bf16[192,2048]{1,0:T(8,128)(2,1)S(1)} collective-permute-done((bf16[192,2048]{1,0:T(8,128)(2,1)S(1)}, bf16[192,2048]{1,0:T(8,128)(2,1)S(1)}, u32[]{:S(2)}, u32[]{:S(2)}) %collective-permute-start.2) | collective-permute-done | bytes 786464 | tf_op jit(solution)/shard_map/ppermute | solution.py:17
  211.1 4.3 copy.20
  215.4 3.2 copy.21
  218.6 64.1 %while.24 = (s32[]{:T(128)}, f32[8,960,128]{2,1,0:T(8,128)}, f32[8,960,768]{2,1,0:T(8,128)}, bf16[8,960,128]{2,1,0:T(8,128)(2,1)S(1)}, bf16[8,768,128]{2,1,0:T(8...) while((s32[]{:T(128)}, f32[8,960,128]{2,1,0:T(8,128)}, ...), condition=%wide.region_3.4_spmd.clone, body=%wide.region_0.3_spmd.clone.sunk | while | flops 387807360 | bytes 18404692 | solution.py:107
  282.7 3.7 convert_element_type.59
  291.7 15.2 %gather_fusion.5 = bf16[192,2,5120]{2,1,0:T(2,128)(2,1)} fusion(bf16[224,2,5120]{2,1,0:T(2,128)(2,1)} %bitcast.26, s32[1024]{0:T(1024)S(1)} %pad_clamp_fusion), kind=kCustom, calls=%fused_computation.5 | custom fusion | bytes 7865088 | tf_op jit(solution)/shard_map/gather | solution.py:62
  306.9 10.4 %copy.25 = bf16[192,2,5120]{0,2,1:T(8,128)(2,1)} copy(bf16[192,2,5120]{2,1,0:T(2,128)(2,1)} %gather_fusion.5) | data formatting | bytes 7864320 | tf_op jit(solution)/shard_map/gather | solution.py:62
  317.3 7.5 %copy.26 = bf16[8,2,5,192,128]{4,3,2,1,0:T(8,128)(2,1)} copy(bf16[8,2,5,192,128]{3,4,2,0,1:T(8,128)(2,1)} %bitcast.155) | data formatting | bytes 7864320 | tf_op jit(solution)/shard_map/transpose | solution.py:120
  324.8 75.7 %while.23 = (s32[]{:T(128)}, f32[8,2,5,128]{3,2,1,0:T(8,128)S(1)}, f32[8,960,768]{2,1,0:T(8,128)}, bf16[8,2,960,128]{3,2,1,0:T(8,128)(2,1)}, bf16[8,768,128]{2,1...) while((s32[]{:T(128)}, f32[8,2,5,128]{3,2,1,0:T(8,128)S(1)}, ...), condition=%wide.region_9.10_spmd, body=%wide.region_4.9_spmd.sunk | while | flops 394437760 | bytes 20058256 | solution.py:123
  400.6 213.1 %psum.7 = f32[2,5120]{1,0:T(2,128)S(1)} all-reduce(f32[2,5120]{1,0:T(2,128)S(1)} %reshape.236), channel_id=1, replica_groups=mesh['dp'=8,'ctx'=32] {'dp','ctx'}, use_global_device_ids=true, to_apply=%region_10.11 | all-reduce | flops 10240 | bytes 81920 | tf_op jit(solution)/shard_map/psum | solution.py:130
  (154 shorter events, 168.2 us)
Async XLA Ops:
  0.6 20.2 %copy-start = (bf16[1,192,5120]{2,1,0:T(8,128)(2,1)S(1)}, bf16[1,192,5120]{2,1,0:T(8,128)(2,1)}, u32[]{:S(2)}) copy-start(bf16[1,192,5120]{2,1,0:T(8,128)(2,1)} %param.10) | copy-start | bytes 5898244
  6.3 36.4 %all-to-all-start.1 = ((bf16[32,7,2048]{2,1,0:T(8,128)(2,1)}), bf16[32,7,2048]{2,1,0:T(8,128)(2,1)S(1)}, u32[]{:S(2)}, u32[]{:S(2)}) async-start(bf16[32,7,2048]{2,1,0:T(8,128)(2,1)} %reshape.254), calls=%async_computation.1 | async-start | bytes 2097152 | tf_op jit(solution)/shard_map/all_to_all | solution.py:66
  42.7 1.0 copy-start.3
  43.7 34.3 %all-to-all-start = ((bf16[32,7,5120]{2,1,0:T(8,128)(2,1)}), bf16[32,7,5120]{2,1,0:T(8,128)(2,1)S(1)}, u32[]{:S(2)}, u32[]{:S(2)}) async-start(bf16[32,7,5120]{2,1,0:T(8,128)(2,1)} %reshape.238), calls=%async_computation | async-start | bytes 5242880 | tf_op jit(solution)/shard_map/all_to_all | solution.py:65
  48.1 18.5 %copy-start.4 = (s32[1,192]{1,0:T(1,128)S(1)}, s32[1,192]{1,0:T(1,128)}, u32[]{:S(2)}) copy-start(s32[1,192]{1,0:T(1,128)} %param.14) | copy-start | bytes 2308
  78.0 1.5 copy-start.2
  79.5 212.2 %all-to-all-start.2 = ((bf16[32,7,2,5120]{3,2,1,0:T(2,128)(2,1)}), bf16[32,7,2,5120]{3,2,1,0:T(2,128)(2,1)}, u32[]{:S(2)}, u32[]{:S(2)}) async-start(bf16[32,7,2,5120]{3,2,1,0:T(2,128)(2,1)} %bitcast.157), calls=%async_computation.2 | async-start | bytes 9175040 | tf_op jit(solution)/shard_map/all_to_all | solution.py:67
  95.3 5.5 copy-start.5
  96.5 89.4 %collective-permute-start = (bf16[192,2048]{1,0:T(8,128)(2,1)S(1)}, bf16[192,2048]{1,0:T(8,128)(2,1)S(1)}, u32[]{:S(2)}, u32[]{:S(2)}) collective-permute-start(bf16[192,2048]{1,0:T(8,128)(2,1)S(1)} %gather_fusion.3), channel_id=1, source_target_pairs={{0,3},{1,4},{2,5},{3,6},{4,7},{5,8},{6,9},{7,10},{8,11},{9,12},{10... | collective-permute-start | bytes 2359304 | tf_op jit(solution)/shard_map/ppermute | solution.py:17
  100.9 66.2 %collective-permute-start.3 = (bf16[192]{0:T(256)(128)(2,1)S(1)}, bf16[192]{0:T(256)(128)(2,1)S(1)}, u32[]{:S(2)}, u32[]{:S(2)}) collective-permute-start(bf16[192]{0:T(256)(128)(2,1)S(1)} %convert_reduce_fusion), channel_id=1, source_target_pairs={{0,3},{1,4},{2,5},{3,6},{4,7},{5,8},{6,9},{7,10},{8,11},{9,12},{10... | collective-permute-start | bytes 1160 | tf_op jit(solution)/shard_map/ppermute | solution.py:17
  108.1 77.5 %collective-permute-start.4 = (bf16[192]{0:T(256)(128)(2,1)S(1)}, bf16[192]{0:T(256)(128)(2,1)S(1)}, u32[]{:S(2)}, u32[]{:S(2)}) collective-permute-start(bf16[192]{0:T(256)(128)(2,1)S(1)} %convert_reduce_fusion), channel_id=1, source_target_pairs={{0,2},{1,3},{2,4},{3,5},{4,6},{5,7},{6,8},{7,9},{8,10},{9,11},{10,... | collective-permute-start | bytes 1160 | tf_op jit(solution)/shard_map/ppermute | solution.py:17
  111.2 74.4 %collective-permute-start.5 = (bf16[192]{0:T(256)(128)(2,1)S(1)}, bf16[192]{0:T(256)(128)(2,1)S(1)}, u32[]{:S(2)}, u32[]{:S(2)}) collective-permute-start(bf16[192]{0:T(256)(128)(2,1)S(1)} %convert_reduce_fusion), channel_id=1, source_target_pairs={{0,1},{1,2},{2,3},{3,4},{4,5},{5,6},{6,7},{7,8},{8,9},{9,10},{10,1... | collective-permute-start | bytes 1160 | tf_op jit(solution)/shard_map/ppermute | solution.py:17
  113.7 72.3 %collective-permute-start.1 = (bf16[192,2048]{1,0:T(8,128)(2,1)S(1)}, bf16[192,2048]{1,0:T(8,128)(2,1)S(1)}, u32[]{:S(2)}, u32[]{:S(2)}) collective-permute-start(bf16[192,2048]{1,0:T(8,128)(2,1)S(1)} %gather_fusion.3), channel_id=1, source_target_pairs={{0,2},{1,3},{2,4},{3,5},{4,6},{5,7},{6,8},{7,9},{8,10},{9,11},{10,... | collective-permute-start | bytes 2359304 | tf_op jit(solution)/shard_map/ppermute | solution.py:17
  167.1 34.6 %collective-permute-start.2 = (bf16[192,2048]{1,0:T(8,128)(2,1)S(1)}, bf16[192,2048]{1,0:T(8,128)(2,1)S(1)}, u32[]{:S(2)}, u32[]{:S(2)}) collective-permute-start(bf16[192,2048]{1,0:T(8,128)(2,1)S(1)} %gather_fusion.3), channel_id=1, source_target_pairs={{0,1},{1,2},{2,3},{3,4},{4,5},{5,6},{6,7},{7,8},{8,9},{9,10},{10,1... | collective-permute-start | bytes 2359304 | tf_op jit(solution)/shard_map/ppermute | solution.py:17
  400.5 213.8 %copy-start.1 = (bf16[1,192,5120]{2,1,0:T(8,128)(2,1)S(1)}, bf16[1,192,5120]{2,1,0:T(8,128)(2,1)}, u32[]{:S(2)}) copy-start(bf16[1,192,5120]{2,1,0:T(8,128)(2,1)} %param.10) | copy-start | bytes 5898244
where the time goes:
time: 617 us; the launch traced here: 614 us
  blocking collectives  213 us (35%)
  local copies, waits for them, and re-layouts  92.9 us (15%)
  matrix products  92.3 us (15%)
  waiting for transfers between devices  89 us (14%)
  starting transfers between devices  74.5 us (12%)
  other arithmetic  51.1 us (8%)
    psum x1, blocking collectives, per_device(): totals = lax.psum(probe_terms, ('dp', 'ctx'))  213 us
    ppermute x6, waiting for transfers between devices, from_behind(): return lax.ppermute(block, axis, route)  63.3 us
    dot_general x16, matrix products, head_backward(): jnp.dot(upstream, value_rows.T, preferred_element_type=jnp.float32)  42.2 us
    ppermute x6, starting transfers between devices, from_behind(): return lax.ppermute(block, axis, route)  41.3 us
    gather x5, local copies, waits for them, and re-layouts, arrange(): return flat_rows[slot_index]  34 us
    dynamic_update_slice x8, other arithmetic, per_device(): lax.map(lambda operands: head_forward(operands[0], operands[1], operands[...  20.9 us
    gather x1, local copies, waits for them, and re-layouts, per_device(): outgoing_upstream = cotangents[0][picked_rows]  18.5 us
    dot_general x8, matrix products, head_forward(): jnp.dot(probabilities.astype(jnp.bfloat16), value_rows, preferred_element...  18.3 us
  transfers between devices with their start and end apart: 9, of which 4 were waited for; matrix products, arithmetic and copies ran while one was open for 19% of the time, Pallas kernels for 0%

commit v1 on v0

v1 whole, which is shorter than its diff:
```python
import functools
import math

import jax
import jax.numpy as jnp
from jax import lax
from jax.experimental import pallas as pl
from jax.experimental.pallas import tpu as pltpu
from jax.sharding import PartitionSpec as P

QUERY_HEADS = 40
KEY_VALUE_HEADS = 8
HEAD_SIZE = 128
TOK = 192
CAP = 7
OWNERS = 32
RING = 4
GROUP = QUERY_HEADS // KEY_VALUE_HEADS
KV_LOCAL = KEY_VALUE_HEADS // RING
Q_COLS = QUERY_HEADS * HEAD_SIZE // RING
K_COLS = KV_LOCAL * HEAD_SIZE
SLOTS = 8 * RING
WINDOW = 4 * TOK
BEHIND = 3 * TOK
VMEM = 60 * 1024 * 1024
MESH = pl.DeviceIdType.MESH
F32 = jnp.float32
BF16 = jnp.bfloat16


def peer(ctx):
    return (lax.axis_index("dp"), ctx)


def spread_kernel(q, kv, cot, meta, qx, cx, kvall, metaall,
                  loc_sem, kvs, kvr, qs, qr, cs, cr, ms, mr, zs, zr, ys, yr, yzs, yzr):
    me = lax.axis_index("ctx")
    x = lax.rem(me, RING)
    base = me - x
    zoff = lax.rem(me // 4, 2)
    zpeer = me + 4 - 8 * zoff
    zbase = zpeer - x
    y = me // 8

    barrier = pltpu.get_barrier_semaphore()

    @pl.loop(1, OWNERS)
    def _(d):
        pl.semaphore_signal(barrier, inc=1, device_id=peer(lax.rem(me + d, OWNERS)), device_id_type=MESH)

    local = [
        pltpu.make_async_copy(kv.at[:, pl.ds(x * K_COLS, K_COLS)], kvall.at[me, :, pl.ds(0, K_COLS)], loc_sem.at[0]),
        pltpu.make_async_copy(
            kv.at[:, pl.ds((RING + x) * K_COLS, K_COLS)], kvall.at[me, :, pl.ds(K_COLS, K_COLS)], loc_sem.at[1]),
        pltpu.make_async_copy(q.at[:, pl.ds(x * Q_COLS, Q_COLS)], qx.at[x], loc_sem.at[2]),
        pltpu.make_async_copy(cot.at[:, :, pl.ds(x * Q_COLS, Q_COLS)], cx.at[x], loc_sem.at[3]),
        pltpu.make_async_copy(meta, metaall.at[me], loc_sem.at[4]),
    ]
    for copy in local:
        copy.start()
    pl.semaphore_wait(barrier, OWNERS - 1)

    def kv_copy(d, half, to):
        g = lax.rem(x + d, RING)
        return pltpu.make_async_remote_copy(
            kv.at[:, pl.ds((half * RING + g) * K_COLS, K_COLS)],
            kvall.at[to, :, pl.ds(half * K_COLS, K_COLS)],
            kvs.at[d, half], kvr.at[d, half], device_id=peer(base + g), device_id_type=MESH)

    def q_copy(d, to):
        g = lax.rem(x + d, RING)
        return pltpu.make_async_remote_copy(
            q.at[:, pl.ds(g * Q_COLS, Q_COLS)], qx.at[to], qs.at[d], qr.at[d],
            device_id=peer(base + g), device_id_type=MESH)

    def c_copy(d, to):
        g = lax.rem(x + d, RING)
        return pltpu.make_async_remote_copy(
            cot.at[:, :, pl.ds(g * Q_COLS, Q_COLS)], cx.at[to], cs.at[d], cr.at[d],
            device_id=peer(base + g), device_id_type=MESH)

    def meta_copy(d, to):
        return pltpu.make_async_remote_copy(
            meta, metaall.at[to], ms.at[d], mr.at[d], device_id=peer(lax.rem(me + d, OWNERS)), device_id_type=MESH)

    def z_copy(i, first):
        return pltpu.make_async_remote_copy(
            kvall.at[first + i], kvall.at[first + i], zs.at[i], zr.at[i], device_id=peer(zpeer), device_id_type=MESH)

    def y_copy(d, first):
        return pltpu.make_async_remote_copy(
            kvall.at[pl.ds(first, RING)], kvall.at[pl.ds(first, RING)], ys.at[d], yr.at[d],
            device_id=peer(lax.rem(me + 8 * d, OWNERS)), device_id_type=MESH)

    def yz_copy(d, i, first):
        return pltpu.make_async_remote_copy(
            kvall.at[first + i], kvall.at[first + i], yzs.at[d, i], yzr.at[d, i],
            device_id=peer(lax.rem(me + 8 * d, OWNERS)), device_id_type=MESH)

    def behind(d):
        return base + lax.rem(x + RING - d, RING)

    def y_base(first, d):
        return lax.rem(first + OWNERS - 8 * d, OWNERS)

    for d in (1, 3, 2):
        for half in range(2):
            kv_copy(d, half, me).start()

    @pl.loop(1, OWNERS)
    def _(d):
        meta_copy(d, me).start()

    local[0].wait()
    local[1].wait()
    for d in (1, 3, 2):
        for half in range(2):
            kv_copy(d, half, behind(d)).wait_recv()
    for i in range(RING):
        z_copy(i, base).start()
    for d in (1, 3, 2):
        y_copy(d, base).start()
    for d in (1, 3, 2):
        q_copy(d, x).start()
    for d in (1, 3, 2):
        c_copy(d, x).start()
    for i in range(RING):
        z_copy(i, zbase).wait_recv()
        for d in (1, 3, 2):
            yz_copy(d, i, zbase).start()
    for copy in local[2:]:
        copy.wait()
    for d in (1, 3, 2):
        q_copy(d, lax.rem(x + RING - d, RING)).wait_recv()
    for d in (1, 3, 2):
        c_copy(d, lax.rem(x + RING - d, RING)).wait_recv()
    for d in (1, 3, 2):
        y_copy(d, y_base(base, d)).wait_recv()
        for i in range(RING):
            yz_copy(d, i, y_base(zbase, d)).wait_recv()

    @pl.loop(1, OWNERS)
    def _(d):
        meta_copy(d, lax.rem(me + OWNERS - d, OWNERS)).wait_recv()
        meta_copy(d, me).wait_send()

    for d in (1, 3, 2):
        for half in range(2):
            kv_copy(d, half, me).wait_send()
        q_copy(d, x).wait_send()
        c_copy(d, x).wait_send()
        y_copy(d, base).wait_send()
        for i in range(RING):
            yz_copy(d, i, zbase).wait_send()
    for i in range(RING):
        z_copy(i, base).wait_send()


def spread(q, kv, cot, meta):
    hbm = pl.BlockSpec(memory_space=pl.ANY)
    dma = pltpu.SemaphoreType.DMA
    return pl.pallas_call(
        spread_kernel,
        out_shape=(
            jax.ShapeDtypeStruct((RING, TOK, Q_COLS), BF16),
            jax.ShapeDtypeStruct((RING, 2, TOK, Q_COLS), BF16),
            jax.ShapeDtypeStruct((OWNERS, TOK, 2 * K_COLS), BF16),
            jax.ShapeDtypeStruct((OWNERS, 8, 256), jnp.int32),
        ),
        in_specs=[hbm] * 4,
        out_specs=(hbm,) * 4,
        scratch_shapes=[
            dma((5,)), dma((RING, 2)), dma((RING, 2)), dma((RING,)), dma((RING,)), dma((RING,)), dma((RING,)),
            dma((OWNERS,)), dma((OWNERS,)), dma((RING,)), dma((RING,)), dma((RING,)), dma((RING,)),
            dma((RING, RING)), dma((RING, RING)),
        ],
        compiler_params=pltpu.CompilerParams(collective_id=0, has_side_effects=True),
        name="spread",
    )(q, kv, cot, meta)


def turned_dot(a, b):
    return lax.dot_general(a, b, (((0,), (0,)), ((), ())), preferred_element_type=F32)


def dot_t(a, b):
    return lax.dot_general(a, b, (((1,), (1,)), ((), ())), preferred_element_type=F32)


def attend_kernel(kind, sbase, q, c, kv, rows, codes, segs, keysegs, out, grads,
                  qslots, cslots, kvslots, kvs, acc):
    row_iota = lax.broadcasted_iota(jnp.int32, (TOK, 256), 0)

    def one_hot(row):
        return jnp.where(row_iota == row, 1.0, 0.0).astype(BF16)

    first = sbase[0]

    def ring_rows(i, carry):
        del carry
        hots = [one_hot(rows[pl.ds(first + 2 * i + j, 1), :]) for j in range(2)]

        def put(ref, parts):
            both = jnp.concatenate([part.reshape(OWNERS, 8, Q_COLS) for part in parts], axis=1)
            ref[:, pl.ds(pl.multiple_of(16 * i, 16), 16), :] = both.astype(BF16)

        put(qslots, [turned_dot(hots[j], q[2 * i + j]) for j in range(2)])
        for p in range(2):
            put(cslots.at[p], [turned_dot(hots[j], c[2 * i + j, p]) for j in range(2)])
        return 0

    lax.fori_loop(0, 2, ring_rows, 0)

    def source_rows(i, carry):
        del carry
        parts = [
            turned_dot(one_hot(rows[pl.ds(2 * i + j, 1), :]), kv[2 * i + j]).reshape(OWNERS, 8, 2 * K_COLS)
            for j in range(2)
        ]
        kvslots[:, pl.ds(pl.multiple_of(16 * i, 16), 16), :] = jnp.concatenate(parts, axis=1).astype(BF16)
        return 0

    lax.fori_loop(0, OWNERS // 2, source_rows, 0)

    acc[...] = jnp.zeros_like(acc)
    kvs[pl.ds(0, BEHIND), :] = jnp.zeros((BEHIND, 2 * K_COLS), BF16)
    code_iota = lax.broadcasted_iota(jnp.int32, (256, TOK), 0)
    slot_code = lax.broadcasted_iota(jnp.int32, (SLOTS, TOK), 0) + first * 8
    own_row = lax.broadcasted_iota(jnp.int32, (SLOTS, TOK), 1)
    scale = 1.0 / math.sqrt(HEAD_SIZE)
    exponent = scale * math.log2(math.e)

    def owner(t, carry):
        del carry
        code = codes[pl.ds(t, 1), :]
        hot = jnp.where(code_iota == code, 1.0, 0.0).astype(BF16)
        kvs[pl.ds(pl.multiple_of(BEHIND + t * TOK, 64), TOK), :] = turned_dot(hot, kvslots[t]).astype(BF16)
        mine = slot_code == code
        row_at = jnp.sum(jnp.where(mine, (own_row + BEHIND).astype(F32), 0.0), axis=1, keepdims=True)
        row_seg = jnp.sum(jnp.where(mine, (segs[pl.ds(t, 1), :] + 1).astype(F32), 0.0), axis=1, keepdims=True) - 1.0

        def attend(width):
            start = pl.multiple_of(BEHIND + (t + 1) * TOK - width, 64)
            key_at = lax.broadcasted_iota(jnp.int32, (SLOTS, width), 1).astype(F32) + float(WINDOW - width)
            key_seg = keysegs[pl.ds(t, 1), WINDOW - width:].astype(F32)
            bias = jnp.where((key_at <= row_at) & (key_seg == row_seg), 0.0, -1e30)
            for a in range(KV_LOCAL):
                cols = a * GROUP * HEAD_SIZE

                def heads(ref):
                    return jnp.concatenate(
                        [ref[t, :, cols + h * HEAD_SIZE: cols + (h + 1) * HEAD_SIZE] for h in range(GROUP)], axis=0)

                keys = kvs[pl.ds(start, width), a * HEAD_SIZE: (a + 1) * HEAD_SIZE]
                values = kvs[pl.ds(start, width), K_COLS + a * HEAD_SIZE: K_COLS + (a + 1) * HEAD_SIZE]
                scores = dot_t(heads(qslots), keys).reshape(GROUP, SLOTS, width) + bias[None]
                top = jnp.max(scores, axis=2, keepdims=True)
                weights = jnp.exp2((scores - top) * exponent)
                probs = weights * (1.0 / jnp.sum(weights, axis=2, keepdims=True))
                mixed = jnp.dot(
                    probs.astype(BF16).reshape(GROUP * SLOTS, width), values, preferred_element_type=F32)
                for h in range(GROUP):
                    out[t, :, cols + h * HEAD_SIZE: cols + (h + 1) * HEAD_SIZE] = (
                        mixed[h * SLOTS: (h + 1) * SLOTS].astype(BF16))
                sums = []
                for p in range(2):
                    up = heads(cslots.at[p])
                    delta = jnp.sum(up.astype(F32) * mixed, axis=1, keepdims=True)
                    prob_grad = dot_t(up, values)
                    grad = probs * (prob_grad - delta).reshape(GROUP, SLOTS, width)
                    sums.append(jnp.sum(grad.reshape(GROUP, SLOTS // 8, 8, width), axis=1).reshape(GROUP * 8, width))
                sums = jnp.concatenate(sums, axis=0)
                high = sums.astype(BF16)
                low = (sums - high.astype(F32)).astype(BF16)
                both = jnp.concatenate([high, low], axis=0)
                acc[a] += jnp.dot(both, keys, preferred_element_type=F32)

        for n, width in enumerate((256, 384, 512, 768)):
            pl.when(kind[t] == n)(functools.partial(attend, width))
        return 0

    lax.fori_loop(0, OWNERS, owner, 0)

    grads[...] = jnp.zeros_like(grads)
    for p in range(2):
        for a in range(KV_LOCAL):
            total = acc[a, pl.ds(p * GROUP * 8, GROUP * 8), :] + acc[a, pl.ds((2 + p) * GROUP * 8, GROUP * 8), :]
            for h in range(GROUP):
                row = jnp.sum(total[h * 8: (h + 1) * 8], axis=0, keepdims=True) * scale
                grads[pl.ds(p * 16 + a * GROUP + h, 1), :] = row


def attend(kind, sbase, q, c, kv, rows, codes, segs, keysegs):
    vmem = pl.BlockSpec(memory_space=pltpu.VMEM)
    smem = pl.BlockSpec(memory_space=pltpu.SMEM)
    return pl.pallas_call(
        attend_kernel,
        out_shape=(
            jax.ShapeDtypeStruct((OWNERS, SLOTS, Q_COLS), BF16),
            jax.ShapeDtypeStruct((32, HEAD_SIZE), F32),
        ),
        in_specs=[smem, smem] + [vmem] * 7,
        out_specs=(vmem, vmem),
        scratch_shapes=[
            pltpu.VMEM((OWNERS, SLOTS, Q_COLS), BF16),
            pltpu.VMEM((2, OWNERS, SLOTS, Q_COLS), BF16),
            pltpu.VMEM((OWNERS, 256, 2 * K_COLS), BF16),
            pltpu.VMEM((BEHIND + OWNERS * TOK, 2 * K_COLS), BF16),
            pltpu.VMEM((KV_LOCAL, 4 * GROUP * 8, HEAD_SIZE), F32),
        ],
        compiler_params=pltpu.CompilerParams(vmem_limit_bytes=VMEM),
        name="attend",
    )(kind, sbase, q, c, kv, rows, codes, segs, keysegs)


def collect_kernel(token_total, slots, grads, owned, curve,
                   parts, yparts, squares, loc_sem, os, orr, gs, gr, ys, yr, xs, xr):
    me = lax.axis_index("ctx")
    dp = lax.axis_index("dp")
    x = lax.rem(me, RING)
    base = me - x
    yz = me // RING
    zoff = lax.rem(yz, 2)
    line = zoff * 8 + dp

    def line_peer(d):
        n = lax.rem(line + d, 16)
        return (lax.rem(n, 8), me + 4 * (n // 8 - zoff))

    barrier = pltpu.get_barrier_semaphore()

    @pl.loop(1, OWNERS)
    def _(d):
        pl.semaphore_signal(barrier, inc=1, device_id=peer(lax.rem(me + d, OWNERS)), device_id_type=MESH)

    @pl.loop(1, 16)
    def _(d):
        pl.semaphore_signal(barrier, inc=1, device_id=line_peer(d), device_id_type=MESH)

    parts[pl.ds(line, 1)] = grads[...][None]
    own = pltpu.make_async_copy(slots.at[me], owned.at[yz, :, pl.ds(x * Q_COLS, Q_COLS)], loc_sem)
    own.start()
    pl.semaphore_wait(barrier, OWNERS - 1 + 15)

    def g_copy(d, at):
        return pltpu.make_async_remote_copy(
            parts.at[at], parts.at[at], gs.at[d], gr.at[d], device_id=line_peer(d), device_id_type=MESH)

    @pl.loop(1, 16)
    def _(d):
        g_copy(d, line).start()

    def o_copy(d, target, source):
        return pltpu.make_async_remote_copy(
            slots.at[target],
            owned.at[source // RING, :, pl.ds(pl.multiple_of(lax.rem(source, RING) * Q_COLS, Q_COLS), Q_COLS)],
            os.at[d], orr.at[d], device_id=peer(target), device_id_type=MESH)

    @pl.loop(1, OWNERS)
    def _(d):
        o_copy(d, lax.rem(me + d, OWNERS), me).start()

    @pl.loop(1, 16)
    def _(d):
        g_copy(d, lax.rem(line + 16 - d, 16)).wait_recv()
        g_copy(d, line).wait_send()

    y = me // 8
    yparts[pl.ds(y, 1)] = jnp.sum(parts[...], axis=0)[None]

    def y_copy(d, at):
        return pltpu.make_async_remote_copy(
            yparts.at[at], yparts.at[at], ys.at[d], yr.at[d],
            device_id=peer(lax.rem(me + 8 * d, OWNERS)), device_id_type=MESH)

    for d in range(1, RING):
        y_copy(d, y).start()
    for d in range(1, RING):
        y_copy(d, lax.rem(y + RING - d, RING)).wait_recv()
        y_copy(d, y).wait_send()
    total = jnp.sum(yparts[...], axis=0)
    squares[pl.ds(x, 1)] = ((total[:16] * total[:16] + total[16:] * total[16:]) / token_total)[None]

    def x_copy(d, at):
        return pltpu.make_async_remote_copy(
            squares.at[at], squares.at[at], xs.at[d], xr.at[d],
            device_id=peer(base + lax.rem(x + d, RING)), device_id_type=MESH)

    for d in range(1, RING):
        x_copy(d, x).start()
    for d in range(1, RING):
        x_copy(d, lax.rem(x + RING - d, RING)).wait_recv()
        x_copy(d, x).wait_send()
    curve[...] = squares[...]

    own.wait()

    @pl.loop(1, OWNERS)
    def _(d):
        o_copy(d, me, lax.rem(me + OWNERS - d, OWNERS)).wait_recv()
        o_copy(d, lax.rem(me + d, OWNERS), me).wait_send()


def collect(slots, grads, token_total):
    hbm = pl.BlockSpec(memory_space=pl.ANY)
    vmem = pl.BlockSpec(memory_space=pltpu.VMEM)
    dma = pltpu.SemaphoreType.DMA
    return pl.pallas_call(
        functools.partial(collect_kernel, token_total),
        out_shape=(
            jax.ShapeDtypeStruct((OWNERS // RING, SLOTS, RING * Q_COLS), BF16),
            jax.ShapeDtypeStruct((RING, 16, HEAD_SIZE), F32),
        ),
        in_specs=[hbm, vmem],
        out_specs=(hbm, vmem),
        scratch_shapes=[
            pltpu.VMEM((16, 32, HEAD_SIZE), F32),
            pltpu.VMEM((RING, 32, HEAD_SIZE), F32),
            pltpu.VMEM((RING, 16, HEAD_SIZE), F32),
            dma, dma((OWNERS,)), dma((OWNERS,)), dma((16,)), dma((16,)),
            dma((RING,)), dma((RING,)), dma((RING,)), dma((RING,)),
        ],
        compiler_params=pltpu.CompilerParams(collective_id=1, has_side_effects=True),
        name="collect",
    )(slots, grads)


def order_kernel(code, slots, out):
    iota = lax.broadcasted_iota(jnp.int32, (256, TOK), 0)
    hot = jnp.where(iota == code[...], 1.0, 0.0).astype(BF16)
    out[...] = turned_dot(hot, slots[...]).astype(BF16)


def order(code, slots):
    return pl.pallas_call(
        order_kernel,
        grid=(RING,),
        out_shape=jax.ShapeDtypeStruct((TOK, RING * Q_COLS), BF16),
        in_specs=[
            pl.BlockSpec((1, TOK), lambda i: (0, 0)),
            pl.BlockSpec((256, Q_COLS), lambda i: (0, i)),
        ],
        out_specs=pl.BlockSpec((TOK, Q_COLS), lambda i: (0, i)),
        name="order",
    )(code, slots)


def per_device(queries, packed_keys_values, cotangents, send_rows, take_slots, segment_ids):
    me = lax.axis_index("ctx")
    code = take_slots + take_slots // CAP
    meta = jnp.concatenate([
        jnp.pad(code, ((0, 0), (0, 256 - TOK))),
        jnp.pad(segment_ids, ((0, 0), (0, 256 - TOK))),
        jnp.pad(send_rows[0, 0], ((0, 0), (0, 8 - CAP)), constant_values=-1).reshape(1, 256),
        jnp.zeros((5, 256), jnp.int32),
    ], axis=0)
    cot = jnp.transpose(cotangents[0], (1, 0, 2))
    qx, cx, kvall, metaall = spread(queries[0], packed_keys_values[0], cot, meta)
    codes = metaall[:, 0, :TOK]
    segs = metaall[:, 1, :TOK]
    rows = metaall[:, 2, :]
    flat = jnp.concatenate([jnp.full((BEHIND,), -2, jnp.int32), segs.reshape(-1)])
    keysegs = jnp.concatenate([flat[i * TOK: i * TOK + OWNERS * TOK].reshape(OWNERS, TOK) for i in range(4)], axis=1)
    starts = jnp.sum(segs.reshape(1, -1) < segs[:, :1], axis=1)
    need = (jnp.arange(OWNERS) + 1) * TOK - starts
    kind = (need > 256).astype(jnp.int32) + (need > 384) + (need > 512)
    sbase = (me - lax.rem(me, RING)).reshape(1)
    slots, grads = attend(kind.astype(jnp.int32), sbase, qx, cx, kvall, rows, codes, segs, keysegs)
    token_total = 2.0 * TOK * OWNERS * lax.axis_size("dp")
    owned, curve = collect(slots, grads, token_total)
    out = order(code, owned.reshape(256, RING * Q_COLS))
    return out[None], curve[:, : QUERY_HEADS // RING].reshape(-1)


def solution(mesh):
    placed = (
        P("dp", "ctx", None),
        P("dp", "ctx", None),
        P("dp", "ctx", None, None),
        P("dp", "ctx", None, None),
        P("dp", "ctx"),
        P("dp", "ctx"),
    )
    return jax.shard_map(
        per_device,
        mesh=mesh,
        in_specs=placed,
        out_specs=(P("dp", "ctx", None), P()),
        check_vma=False,
    )
```

time: 617 us -> 252 us (0.41)
  Pallas kernels: 0 us -> 238 us
  blocking collectives: 213 us -> 0 us
  matrix products: 92.3 us -> 0 us
  waiting for transfers between devices: 89 us -> 0 us
  local copies, waits for them, and re-layouts: 92.9 us -> 9.4 us
  starting transfers between devices: 74.5 us -> 0 us
  other arithmetic: 51.1 us -> 3.59 us
    pallas_call x0 -> x4, Pallas kernels: none -> 238 us  [the longest x1 94.3 us: spread(): pl.pallas_call(spread_kernel, out_shape=(jax.ShapeDtypeStruct((RING, TOK,...]
    psum x1 -> x0, blocking collectives: 213 us -> none  [per_device(): totals = lax.psum(probe_terms, ('dp', 'ctx'))]
    dot_general x48 -> x0, matrix products: 92.3 us -> none  [the longest x16 42.2 us: head_backward(): jnp.dot(upstream, value_rows.T, preferred_element_type=jnp.float32)]
    gather x10 -> x0, local copies, waits for them, and re-layouts: 64.7 us -> none  [the longest x5 34 us: arrange(): return flat_rows[slot_index]]
    ppermute x6 -> x0, waiting for transfers between devices: 63.3 us -> none  [from_behind(): return lax.ppermute(block, axis, route)]
    ppermute x6 -> x0, starting transfers between devices: 41.3 us -> none  [from_behind(): return lax.ppermute(block, axis, route)]
    all_to_all x3 -> x0, starting transfers between devices: 33.2 us -> none  [the longest x1 14.5 us: per_device(): lax.all_to_all(outgoing_pairs, 'ctx', split_axis=0, concat_axis=0, tiled=...]
    all_to_all x3 -> x0, waiting for transfers between devices: 25.7 us -> none  [the longest x1 14.3 us: per_device(): lax.all_to_all(outgoing_pairs, 'ctx', split_axis=0, concat_axis=0, tiled=...]
  transfers between devices with their start and end apart: 9 -> 0, of which waited for: 4 -> 0; matrix products, arithmetic and copies ran while one was open for 19% -> 0% of each run, Pallas kernels for 0% -> 0%
where the time goes in v1:
time: 252 us; the launch traced here: 251 us
  Pallas kernels  238 us (94%)
  local copies, waits for them, and re-layouts  9.4 us (4%)
  other arithmetic  3.59 us (1%)
    pallas_call x1, Pallas kernels, spread(): pl.pallas_call(spread_kernel, out_shape=(jax.ShapeDtypeStruct((RING, TOK,...  94.3 us
    pallas_call x1, Pallas kernels, collect(): pl.pallas_call(functools.partial(collect_kernel, token_total), out_shape=...  77.5 us
    pallas_call x1, Pallas kernels, attend(): pl.pallas_call(attend_kernel, out_shape=(jax.ShapeDtypeStruct((OWNERS, SL...  61.5 us
    unnamed x8, local copies, waits for them, and re-layouts  5.86 us

profile of v1, /device:TPU:1, one launch (start us, length us, event | category | flops | bytes accessed | tf_op | source)
XLA Modules:
  0.0 251.4 jit_solution(1312315168122260204)
XLA Ops:
  0.6 0.7 fusion.2.code
  1.3 0.0 copy-start.2
  1.3 0.8 copy.25
  2.1 0.1 reshape.50
  2.2 0.1 pad.22.clone
  2.3 1.3 fusion.1.meta
  3.6 5.1 %copy.27 = bf16[1,192,2,5120]{3,1,2,0:T(8,128)(2,1)} copy(bf16[1,192,2,5120]{3,2,1,0:T(2,128)(2,1)} %param.8) | data formatting | bytes 7864320 | tf_op args[2]
  8.7 94.3 %spread.1 = (bf16[4,192,1280]{2,1,0:T(8,128)(2,1)}, bf16[4,2,192,1280]{3,2,1,0:T(8,128)(2,1)}, bf16[32,192,512]{2,1,0:T(8,128)(2,1)}, s32[32,8,256]{2,1,0:T(8,128)}) custom-call(bf16[192,5120]{1,0:T(8,128)(2,1)} %bitcast.24, bf16[192,2048]{1,0:T(8,128)(2,1)} %bitcast.25, bf16[2,192,5120]{2,1,0:T(8,128)(2,1)} %bitcast.21, s32[8,256]{1,0:T(8,128)} %fusion.1.meta), custom_call_target="tpu_custom_call" | custom-call | tf_op jit(solution)/shard_map/spread/pallas_call | solution.py:162
  103.0 1.0 copy.20
  104.0 0.6 slice_bitcast_fusion
  104.7 0.1 lt.17
  104.7 0.1 pad_slice_fusion.2
  104.8 0.1 reshape.52
  104.9 0.1 reshape.53
  105.0 0.1 reshape.54
  105.0 0.7 pad_add_fusion.keysegs
  105.8 0.1 slice_reduce_fusion
  105.9 0.3 convert_reduce_fusion
  106.2 0.5 fusion.4.kind
  106.7 0.6 slice_bitcast_fusion.1.rows
  107.3 61.5 %attend.1 = (bf16[32,32,1280]{2,1,0:T(8,128)(2,1)}, f32[32,128]{1,0:T(8,128)}) custom-call(s32[32]{0:T(128)} %fusion.4.kind, s32[1]{0:T(128)} %bitcast.5.sbase, bf16[4,192,1280]{2,1,0:T(8,128)(2,1)} %get-tuple-element.11.q, bf16[4,2,192,1280]{3,2,1,0:T(8,128)(2,1)} %get-tuple-element.12.c, bf16[32,192,512]{2,1,0:T(8,128)(2,1)} %get-tuple-element.13.kv, ...), custom_call_target="tpu_custom_call" | custom-call | tf_op jit(solution)/shard_map/attend/pallas_call | solution.py:296
  168.8 77.5 %collect.1 = (bf16[8,32,5120]{2,1,0:T(8,128)(2,1)}, f32[4,16,128]{2,1,0:T(8,128)}) custom-call(bf16[32,32,1280]{2,1,0:T(8,128)(2,1)} %get-tuple-element.14.slots, f32[32,128]{1,0:T(8,128)} %get-tuple-element.15.grads), custom_call_target="tpu_custom_call" | custom-call | tf_op jit(solution)/shard_map/collect/pallas_call | solution.py:408
  246.3 4.4 %order.1 = bf16[192,5120]{1,0:T(8,128)(2,1)} custom-call(s32[1,192]{1,0:T(1,128)} %copy-done.2, bf16[256,5120]{1,0:T(8,128)(2,1)} %bitcast.22), custom_call_target="tpu_custom_call" | custom-call | tf_op jit(solution)/shard_map/order/pallas_call | solution.py:435
  250.8 0.6 reshape.56
  (7 shorter events, 0.0 us)
Async XLA Ops:
  1.3 7.4 %copy-start.2 = (s32[1,192]{1,0:T(1,128)}, s32[1,192]{1,0:T(1,128)S(1)}, u32[]{:S(2)}) copy-start(s32[1,192]{1,0:T(1,128)S(1)} %fusion.2.code) | copy-start | bytes 2308
  104.7 2.7 %copy-start = (s32[32,192]{1,0:T(8,128)}, s32[32,192]{1,0:T(8,128)S(1)}, u32[]{:S(2)}) copy-start(s32[32,192]{1,0:T(8,128)S(1)} %get-tuple-element.19.segs) | copy-start | bytes 73732
  246.3 4.5 %copy-start.1 = (f32[4,16,128]{2,1,0:T(8,128)S(1)}, f32[4,16,128]{2,1,0:T(8,128)}, u32[]{:S(2)}) copy-start(f32[4,16,128]{2,1,0:T(8,128)} %get-tuple-element.17) | copy-start | bytes 98308

commit v2 on v0

v2 whole, which is shorter than its diff:
```python
import functools
import math

import jax
import jax.numpy as jnp
from jax import lax
from jax.experimental import pallas as pl
from jax.experimental.pallas import tpu as pltpu
from jax.sharding import PartitionSpec as P

QUERY_HEADS = 40
KEY_VALUE_HEADS = 8
HEAD_SIZE = 128
TOK = 192
CAP = 7
OWNERS = 32
RING = 4
GROUP = QUERY_HEADS // KEY_VALUE_HEADS
KV_LOCAL = KEY_VALUE_HEADS // RING
Q_COLS = QUERY_HEADS * HEAD_SIZE // RING
A_COLS = GROUP * HEAD_SIZE
K_COLS = KV_LOCAL * HEAD_SIZE
SLOTS = 8 * RING
WINDOW = 4 * TOK
BEHIND = 3 * TOK
LINE = 16
VMEM = 60 * 1024 * 1024
MESH = pl.DeviceIdType.MESH
F32 = jnp.float32
BF16 = jnp.bfloat16


def turned_dot(a, b):
    return lax.dot_general(a, b, (((0,), (0,)), ((), ())), preferred_element_type=F32)


def dot_t(a, b):
    return lax.dot_general(a, b, (((1,), (1,)), ((), ())), preferred_element_type=F32)


def one_hot(row, count):
    iota = lax.broadcasted_iota(jnp.int32, (count, row.shape[1]), 0)
    return jnp.where(iota == row, 1.0, 0.0).astype(BF16)


def peer(ctx):
    return (lax.axis_index("dp"), ctx)


def kernel(token_total, q, kv, cot, meta, result, curve,
           qbuf, cbuf, kvbuf, metaall, qslots, cslots, kvslots, kvs, bias, slots, owned, acc, grads,
           parts, yparts, squares,
           loc, kvsend, kvrecv, qsend, qrecv, csend, crecv, msend, mrecv, zsend, zrecv, ysend, yrecv, yzsend, yzrecv,
           osend, orecv, gsend, grecv, bsend, brecv, xsend, xrecv):
    me = lax.axis_index("ctx")
    dp = lax.axis_index("dp")
    x = lax.rem(me, RING)
    base = me - x
    yz = me // RING
    zoff = lax.rem(yz, 2)
    y = me // 8
    zpeer = me + 4 - 8 * zoff
    zbase = zpeer - x
    line = zoff * 8 + dp
    directions = (1, 3, 2)
    scale = 1.0 / math.sqrt(HEAD_SIZE)
    exponent = scale * math.log2(math.e)

    def line_peer(d):
        n = lax.rem(line + d, LINE)
        return (lax.rem(n, 8), me + 4 * (n // 8 - zoff))

    def up(d):
        return lax.rem(x + d, RING)

    def down(d):
        return lax.rem(x + RING - d, RING)

    def y_base(first, d):
        return lax.rem(first + OWNERS - 8 * d, OWNERS)

    def kv_copy(a, d, half, to):
        return pltpu.make_async_remote_copy(
            kv.at[:, pl.ds((half * RING + up(d)) * K_COLS + a * HEAD_SIZE, HEAD_SIZE)],
            kvbuf.at[a, to, :, pl.ds(half * HEAD_SIZE, HEAD_SIZE)],
            kvsend.at[a, d, half], kvrecv.at[a, d, half], device_id=peer(base + up(d)), device_id_type=MESH)

    def q_copy(a, d, to):
        return pltpu.make_async_remote_copy(
            q.at[:, pl.ds(up(d) * Q_COLS + a * A_COLS, A_COLS)], qbuf.at[a, to], qsend.at[a, d], qrecv.at[a, d],
            device_id=peer(base + up(d)), device_id_type=MESH)

    def c_copy(a, d, to):
        return pltpu.make_async_remote_copy(
            cot.at[:, :, pl.ds(up(d) * Q_COLS + a * A_COLS, A_COLS)], cbuf.at[a, to], csend.at[a, d], crecv.at[a, d],
            device_id=peer(base + up(d)), device_id_type=MESH)

    def meta_copy(d, to):
        return pltpu.make_async_remote_copy(
            meta, metaall.at[3 + to], msend.at[d], mrecv.at[d],
            device_id=peer(lax.rem(me + d, OWNERS)), device_id_type=MESH)

    def z_copy(a, i, first):
        return pltpu.make_async_remote_copy(
            kvbuf.at[a, first + i], kvbuf.at[a, first + i], zsend.at[a, i], zrecv.at[a, i],
            device_id=peer(zpeer), device_id_type=MESH)

    def y_copy(a, d, first):
        return pltpu.make_async_remote_copy(
            kvbuf.at[a, pl.ds(first, RING)], kvbuf.at[a, pl.ds(first, RING)], ysend.at[a, d], yrecv.at[a, d],
            device_id=peer(lax.rem(me + 8 * d, OWNERS)), device_id_type=MESH)

    def yz_copy(a, d, i, first):
        return pltpu.make_async_remote_copy(
            kvbuf.at[a, first + i], kvbuf.at[a, first + i], yzsend.at[a, d, i], yzrecv.at[a, d, i],
            device_id=peer(lax.rem(me + 8 * d, OWNERS)), device_id_type=MESH)

    def o_copy(a, d, target, source):
        return pltpu.make_async_remote_copy(
            slots.at[a, target],
            owned.at[source // RING, :, pl.ds(pl.multiple_of(lax.rem(source, RING) * Q_COLS + a * A_COLS, 128), A_COLS)],
            osend.at[a, d], orecv.at[a, d], device_id=peer(target), device_id_type=MESH)

    def kv_local(a, half):
        return pltpu.make_async_copy(
            kv.at[:, pl.ds((half * RING + x) * K_COLS + a * HEAD_SIZE, HEAD_SIZE)],
            kvbuf.at[a, me, :, pl.ds(half * HEAD_SIZE, HEAD_SIZE)], loc.at[a, half])

    def q_local(a):
        return pltpu.make_async_copy(q.at[:, pl.ds(x * Q_COLS + a * A_COLS, A_COLS)], qbuf.at[a, x], loc.at[a, 2])

    def c_local(a):
        return pltpu.make_async_copy(
            cot.at[:, :, pl.ds(x * Q_COLS + a * A_COLS, A_COLS)], cbuf.at[a, x], loc.at[a, 3])

    def o_local(a):
        return pltpu.make_async_copy(
            slots.at[a, me], owned.at[yz, :, pl.ds(pl.multiple_of(x * Q_COLS + a * A_COLS, 128), A_COLS)], loc.at[a, 4])

    meta_local = pltpu.make_async_copy(meta, metaall.at[3 + me], loc.at[0, 5])

    barrier = pltpu.get_barrier_semaphore()

    @pl.loop(1, OWNERS)
    def _(d):
        pl.semaphore_signal(barrier, inc=1, device_id=peer(lax.rem(me + d, OWNERS)), device_id_type=MESH)

    @pl.loop(1, LINE)
    def _(d):
        pl.semaphore_signal(barrier, inc=1, device_id=line_peer(d), device_id_type=MESH)

    meta_local.start()
    for a in range(KV_LOCAL):
        for half in range(2):
            kv_local(a, half).start()
        q_local(a).start()
        c_local(a).start()
    metaall[pl.ds(0, 3)] = jnp.zeros((3, 8, 256), jnp.int32)
    acc[...] = jnp.zeros_like(acc)
    for a in range(KV_LOCAL):
        kvs[a, pl.ds(0, BEHIND), :] = jnp.zeros((BEHIND, 2 * HEAD_SIZE), BF16)
    pl.semaphore_wait(barrier, OWNERS - 1 + LINE - 1)

    for a in range(KV_LOCAL):
        for d in directions:
            for half in range(2):
                kv_copy(a, d, half, me).start()

    @pl.loop(1, OWNERS)
    def _(d):
        meta_copy(d, me).start()

    for d in directions:
        q_copy(0, d, x).start()
    for d in directions:
        c_copy(0, d, x).start()

    def pair_rows(a, i):
        parts_ = [
            turned_dot(one_hot(metaall[3 + 2 * i + j][2:3], TOK), kvbuf[a, 2 * i + j])
            .reshape(OWNERS, 8, 2 * HEAD_SIZE) for j in range(2)
        ]
        kvslots[a, :, pl.ds(pl.multiple_of(16 * i, 16), 16), :] = jnp.concatenate(parts_, axis=1).astype(BF16)

    def ring_rows(a, first):
        for i in range(2):
            pair_rows(a, first // 2 + i)

    def ring_into(a, buf, put):
        @pl.loop(0, 2)
        def _(i):
            parts_ = [
                turned_dot(one_hot(metaall[3 + base + 2 * i + j][2:3], TOK), buf(2 * i + j))
                .reshape(OWNERS, 8, A_COLS) for j in range(2)
            ]
            put[:, pl.ds(pl.multiple_of(16 * i, 16), 16), :] = jnp.concatenate(parts_, axis=1).astype(BF16)

    def wait_kv(a):
        for half in range(2):
            kv_local(a, half).wait()
        for d in directions:
            for half in range(2):
                kv_copy(a, d, half, base + down(d)).wait_recv()

    wait_kv(0)
    for i in range(RING):
        z_copy(0, i, base).start()
    for d in directions:
        y_copy(0, d, base).start()
    wait_kv(1)
    for i in range(RING):
        z_copy(1, i, base).start()

    meta_local.wait()

    @pl.loop(1, OWNERS)
    def _(d):
        meta_copy(d, lax.rem(me + OWNERS - d, OWNERS)).wait_recv()

    ring_rows(0, base)

    slot_code = lax.broadcasted_iota(jnp.int32, (SLOTS, TOK), 0) + base * 8
    own_row = lax.broadcasted_iota(jnp.int32, (SLOTS, TOK), 1) + BEHIND
    key_at = lax.broadcasted_iota(jnp.int32, (SLOTS, WINDOW), 1).astype(F32)

    @pl.loop(0, OWNERS)
    def _(t):
        block = metaall[3 + t]
        mine = slot_code == block[0:1, :TOK]
        row_at = jnp.sum(jnp.where(mine, own_row.astype(F32), 0.0), axis=1, keepdims=True)
        row_seg = jnp.sum(jnp.where(mine, block[1:2, :TOK].astype(F32), 0.0), axis=1, keepdims=True)
        key_seg = jnp.zeros((8, WINDOW), jnp.int32)
        for j in range(4):
            wide = jnp.concatenate([metaall[t + j], jnp.zeros((8, WINDOW - 256), jnp.int32)], axis=1)
            key_seg += wide if j == 0 else pltpu.roll(wide, j * TOK, 1)
        allowed = (key_at <= row_at) & (key_seg[1:2].astype(F32) == row_seg)
        bias[t] = jnp.where(allowed, 0.0, -1e30)

    for i in range(RING):
        z_copy(0, i, zbase).wait_recv()
        for d in directions:
            yz_copy(0, d, i, zbase).start()
    for d in directions:
        y_copy(1, d, base).start()
    ring_rows(0, zbase)
    ring_rows(1, base)

    q_local(0).wait()
    for d in directions:
        q_copy(0, d, down(d)).wait_recv()
        q_copy(1, d, x).start()
    ring_into(0, lambda s: qbuf[0, s], qslots)

    for i in range(RING):
        z_copy(1, i, zbase).wait_recv()
        for d in directions:
            yz_copy(1, d, i, zbase).start()
    ring_rows(1, zbase)

    def rest_of_keys(a):
        for d in directions:
            y_copy(a, d, y_base(base, d)).wait_recv()
            ring_rows(a, y_base(base, d))
        for d in directions:
            for i in range(RING):
                yz_copy(a, d, i, y_base(zbase, d)).wait_recv()
            ring_rows(a, y_base(zbase, d))

        @pl.loop(0, OWNERS)
        def _(t):
            hot = one_hot(metaall[3 + t][0:1, :TOK], 256)
            kvs[a, pl.ds(pl.multiple_of(BEHIND + t * TOK, 64), TOK), :] = turned_dot(hot, kvslots[a, t]).astype(BF16)

    def attend(a, d, u):
        t = lax.rem(me + d, OWNERS)
        start = pl.multiple_of(t * TOK, 64)

        def heads(ref):
            return jnp.concatenate([ref[t, :, h * HEAD_SIZE: (h + 1) * HEAD_SIZE] for h in range(GROUP)], axis=0)

        keys = kvs[a, pl.ds(start, WINDOW), :HEAD_SIZE]
        values = kvs[a, pl.ds(start, WINDOW), HEAD_SIZE:]
        scores = dot_t(heads(qslots), keys).reshape(GROUP, SLOTS, WINDOW) + bias[t][None]
        top = jnp.max(scores, axis=2, keepdims=True)
        weights = jnp.exp2((scores - top) * exponent)
        probs = weights * (1.0 / jnp.sum(weights, axis=2, keepdims=True))
        mixed = jnp.dot(probs.astype(BF16).reshape(GROUP * SLOTS, WINDOW), values, preferred_element_type=F32)
        for h in range(GROUP):
            slots[a, t, :, h * HEAD_SIZE: (h + 1) * HEAD_SIZE] = mixed[h * SLOTS: (h + 1) * SLOTS].astype(BF16)
        sums = []
        for p in range(2):
            upstream = heads(cslots.at[p])
            delta = jnp.sum(upstream.astype(F32) * mixed, axis=1, keepdims=True)
            grad = probs * (dot_t(upstream, values) - delta).reshape(GROUP, SLOTS, WINDOW)
            sums.append(jnp.sum(grad.reshape(GROUP, SLOTS // 8, 8, WINDOW), axis=1).reshape(GROUP * 8, WINDOW))
        sums = jnp.concatenate(sums, axis=0)
        high = sums.astype(BF16)
        low = (sums - high.astype(F32)).astype(BF16)
        acc[a, u] += jnp.dot(jnp.concatenate([high, low], axis=0), keys, preferred_element_type=F32)

    def attend_all(a):
        @pl.loop(0, OWNERS // 2)
        def _(i):
            for u in range(2):
                attend(a, 2 * i + u, u)

            @pl.when(i == 0)
            def _():
                o_local(a).start()

            @pl.when(i > 0)
            def _():
                o_copy(a, 2 * i, lax.rem(me + 2 * i, OWNERS), me).start()

            o_copy(a, 2 * i + 1, lax.rem(me + 2 * i + 1, OWNERS), me).start()

    rest_of_keys(0)
    c_local(0).wait()
    for d in directions:
        c_copy(0, d, down(d)).wait_recv()
        c_copy(1, d, x).start()
    for p in range(2):
        ring_into(0, lambda s, p=p: cbuf[0, s, p], cslots.at[p])
    attend_all(0)

    rest_of_keys(1)
    q_local(1).wait()
    for d in directions:
        q_copy(1, d, down(d)).wait_recv()
    ring_into(1, lambda s: qbuf[1, s], qslots)
    c_local(1).wait()
    for d in directions:
        c_copy(1, d, down(d)).wait_recv()
    for p in range(2):
        ring_into(1, lambda s, p=p: cbuf[1, s, p], cslots.at[p])
    attend_all(1)

    grads[...] = jnp.zeros_like(grads)
    for a in range(KV_LOCAL):
        both = acc[a, 0] + acc[a, 1]
        for p in range(2):
            total = both[p * GROUP * 8: (p + 1) * GROUP * 8] + both[(2 + p) * GROUP * 8: (3 + p) * GROUP * 8]
            for h in range(GROUP):
                row = jnp.sum(total[h * 8: (h + 1) * 8], axis=0, keepdims=True) * scale
                grads[pl.ds(p * 16 + a * GROUP + h, 1), :] = row
    parts[pl.ds(line, 1)] = grads[...][None]

    def g_copy(d, at):
        return pltpu.make_async_remote_copy(
            parts.at[at], parts.at[at], gsend.at[d], grecv.at[d], device_id=line_peer(d), device_id_type=MESH)

    @pl.loop(1, LINE)
    def _(d):
        g_copy(d, line).start()

    @pl.loop(1, LINE)
    def _(d):
        g_copy(d, lax.rem(line + LINE - d, LINE)).wait_recv()
        g_copy(d, line).wait_send()

    yparts[pl.ds(y, 1)] = jnp.sum(parts[...], axis=0)[None]

    def b_copy(d, at):
        return pltpu.make_async_remote_copy(
            yparts.at[at], yparts.at[at], bsend.at[d], brecv.at[d],
            device_id=peer(lax.rem(me + 8 * d, OWNERS)), device_id_type=MESH)

    for d in directions:
        b_copy(d, y).start()
    for d in directions:
        b_copy(d, lax.rem(y + RING - d, RING)).wait_recv()
        b_copy(d, y).wait_send()
    total = jnp.sum(yparts[...], axis=0)
    squares[pl.ds(x, 1)] = ((total[:16] * total[:16] + total[16:] * total[16:]) / token_total)[None]

    def x_copy(d, at):
        return pltpu.make_async_remote_copy(
            squares.at[at], squares.at[at], xsend.at[d], xrecv.at[d],
            device_id=peer(base + up(d)), device_id_type=MESH)

    for d in directions:
        x_copy(d, x).start()
    for d in directions:
        x_copy(d, down(d)).wait_recv()
        x_copy(d, x).wait_send()
    curve[...] = squares[...]

    hot = one_hot(metaall[3 + me][0:1, :TOK], 256)
    for a in range(KV_LOCAL):
        o_local(a).wait()

        @pl.loop(1, OWNERS)
        def _(d):
            o_copy(a, d, me, lax.rem(me + OWNERS - d, OWNERS)).wait_recv()

    for i in range(RING):
        cols = pl.ds(i * Q_COLS, Q_COLS)
        result[:, cols] = turned_dot(hot, owned[:, :, cols].reshape(256, Q_COLS)).astype(BF16)

    @pl.loop(1, OWNERS)
    def _(d):
        meta_copy(d, me).wait_send()
        for a in range(KV_LOCAL):
            o_copy(a, d, lax.rem(me + d, OWNERS), me).wait_send()

    for a in range(KV_LOCAL):
        for d in directions:
            for half in range(2):
                kv_copy(a, d, half, me).wait_send()
            q_copy(a, d, x).wait_send()
            c_copy(a, d, x).wait_send()
            y_copy(a, d, base).wait_send()
            for i in range(RING):
                yz_copy(a, d, i, zbase).wait_send()
        for i in range(RING):
            z_copy(a, i, base).wait_send()


def run(q, kv, cot, meta, token_total):
    hbm = pl.BlockSpec(memory_space=pl.ANY)
    vmem = pl.BlockSpec(memory_space=pltpu.VMEM)
    dma = pltpu.SemaphoreType.DMA
    return pl.pallas_call(
        functools.partial(kernel, token_total),
        out_shape=(
            jax.ShapeDtypeStruct((TOK, RING * Q_COLS), BF16),
            jax.ShapeDtypeStruct((RING, 16, HEAD_SIZE), F32),
        ),
        in_specs=[hbm] * 4,
        out_specs=(vmem, vmem),
        scratch_shapes=[
            pltpu.VMEM((KV_LOCAL, RING, TOK, A_COLS), BF16),
            pltpu.VMEM((KV_LOCAL, RING, 2, TOK, A_COLS), BF16),
            pltpu.VMEM((KV_LOCAL, OWNERS, TOK, 2 * HEAD_SIZE), BF16),
            pltpu.VMEM((3 + OWNERS, 8, 256), jnp.int32),
            pltpu.VMEM((OWNERS, SLOTS, A_COLS), BF16),
            pltpu.VMEM((2, OWNERS, SLOTS, A_COLS), BF16),
            pltpu.VMEM((KV_LOCAL, OWNERS, 256, 2 * HEAD_SIZE), BF16),
            pltpu.VMEM((KV_LOCAL, BEHIND + OWNERS * TOK, 2 * HEAD_SIZE), BF16),
            pltpu.VMEM((OWNERS, SLOTS, WINDOW), F32),
            pltpu.VMEM((KV_LOCAL, OWNERS, SLOTS, A_COLS), BF16),
            pltpu.VMEM((OWNERS // RING, SLOTS, RING * Q_COLS), BF16),
            pltpu.VMEM((KV_LOCAL, 2, 4 * GROUP * 8, HEAD_SIZE), F32),
            pltpu.VMEM((32, HEAD_SIZE), F32),
            pltpu.VMEM((LINE, 32, HEAD_SIZE), F32),
            pltpu.VMEM((RING, 32, HEAD_SIZE), F32),
            pltpu.VMEM((RING, 16, HEAD_SIZE), F32),
            dma((KV_LOCAL, 6)),
            dma((KV_LOCAL, RING, 2)), dma((KV_LOCAL, RING, 2)),
            dma((KV_LOCAL, RING)), dma((KV_LOCAL, RING)), dma((KV_LOCAL, RING)), dma((KV_LOCAL, RING)),
            dma((OWNERS,)), dma((OWNERS,)),
            dma((KV_LOCAL, RING)), dma((KV_LOCAL, RING)), dma((KV_LOCAL, RING)), dma((KV_LOCAL, RING)),
            dma((KV_LOCAL, RING, RING)), dma((KV_LOCAL, RING, RING)),
            dma((KV_LOCAL, OWNERS)), dma((KV_LOCAL, OWNERS)),
            dma((LINE,)), dma((LINE,)), dma((RING,)), dma((RING,)), dma((RING,)), dma((RING,)),
        ],
        compiler_params=pltpu.CompilerParams(collective_id=0, has_side_effects=True, vmem_limit_bytes=VMEM),
        name="curvature",
    )(q, kv, cot, meta)


def per_device(queries, packed_keys_values, cotangents, send_rows, take_slots, segment_ids):
    meta = jnp.concatenate([
        jnp.pad(take_slots + take_slots // CAP, ((0, 0), (0, 256 - TOK))),
        jnp.pad(segment_ids + 1, ((0, 0), (0, 256 - TOK))),
        jnp.pad(send_rows[0, 0], ((0, 0), (0, 8 - CAP)), constant_values=-1).reshape(1, 256),
        jnp.zeros((5, 256), jnp.int32),
    ], axis=0)
    cot = jnp.transpose(cotangents[0], (1, 0, 2))
    token_total = 2.0 * TOK * OWNERS * lax.axis_size("dp")
    out, curve = run(queries[0], packed_keys_values[0], cot, meta, token_total)
    return out[None], curve[:, : QUERY_HEADS // RING].reshape(-1)


def solution(mesh):
    placed = (
        P("dp", "ctx", None),
        P("dp", "ctx", None),
        P("dp", "ctx", None, None),
        P("dp", "ctx", None, None),
        P("dp", "ctx"),
        P("dp", "ctx"),
    )
    return jax.shard_map(
        per_device,
        mesh=mesh,
        in_specs=placed,
        out_specs=(P("dp", "ctx", None), P()),
        check_vma=False,
    )
```

time: 617 us -> 178 us (0.29)
  blocking collectives: 213 us -> 0 us
  Pallas kernels: 0 us -> 164 us
  matrix products: 92.3 us -> 0 us
  waiting for transfers between devices: 89 us -> 0 us
  local copies, waits for them, and re-layouts: 92.9 us -> 10.2 us
  starting transfers between devices: 74.5 us -> 0 us
  other arithmetic: 51.1 us -> 1.38 us
    psum x1 -> x0, blocking collectives: 213 us -> none  [per_device(): totals = lax.psum(probe_terms, ('dp', 'ctx'))]
    pallas_call x0 -> x1, Pallas kernels: none -> 164 us  [run(): pl.pallas_call(functools.partial(kernel, token_total), out_shape=(jax.Sha...]
    dot_general x48 -> x0, matrix products: 92.3 us -> none  [the longest x16 42.2 us: head_backward(): jnp.dot(upstream, value_rows.T, preferred_element_type=jnp.float32)]
    gather x10 -> x0, local copies, waits for them, and re-layouts: 64.7 us -> none  [the longest x5 34 us: arrange(): return flat_rows[slot_index]]
    ppermute x6 -> x0, waiting for transfers between devices: 63.3 us -> none  [from_behind(): return lax.ppermute(block, axis, route)]
    ppermute x6 -> x0, starting transfers between devices: 41.3 us -> none  [from_behind(): return lax.ppermute(block, axis, route)]
    all_to_all x3 -> x0, starting transfers between devices: 33.2 us -> none  [the longest x1 14.5 us: per_device(): lax.all_to_all(outgoing_pairs, 'ctx', split_axis=0, concat_axis=0, tiled=...]
    all_to_all x3 -> x0, waiting for transfers between devices: 25.7 us -> none  [the longest x1 14.3 us: per_device(): lax.all_to_all(outgoing_pairs, 'ctx', split_axis=0, concat_axis=0, tiled=...]
  transfers between devices with their start and end apart: 9 -> 0, of which waited for: 4 -> 0; matrix products, arithmetic and copies ran while one was open for 19% -> 0% of each run, Pallas kernels for 0% -> 0%
where the time goes in v2:
time: 178 us; the launch traced here: 176 us
  Pallas kernels  164 us (92%)
  local copies, waits for them, and re-layouts  10.2 us (6%)
    pallas_call x1, Pallas kernels, run(): pl.pallas_call(functools.partial(kernel, token_total), out_shape=(jax.Sha...  164 us
    unnamed x3, local copies, waits for them, and re-layouts  8.66 us

profile of v2, /device:TPU:1, one launch (start us, length us, event | category | flops | bytes accessed | tf_op | source)
XLA Modules:
  0.0 176.0 jit_solution(14390879894310026179)
XLA Ops:
  0.6 0.1 pad.17.clone
  0.7 0.7 fusion.2
  1.4 0.8 copy.14
  2.2 0.1 reshape.10
  2.3 0.7 fusion.1.meta
  3.0 4.9 %copy.16 = bf16[1,192,2,5120]{3,1,2,0:T(8,128)(2,1)} copy(bf16[1,192,2,5120]{3,2,1,0:T(2,128)(2,1)} %param.8) | data formatting | bytes 7864320 | tf_op args[2]
  7.9 163.8 %curvature.1 = (bf16[192,5120]{1,0:T(8,128)(2,1)}, f32[4,16,128]{2,1,0:T(8,128)}) custom-call(bf16[192,5120]{1,0:T(8,128)(2,1)} %bitcast.12, bf16[192,2048]{1,0:T(8,128)(2,1)} %bitcast.14, bf16[2,192,5120]{2,1,0:T(8,128)(2,1)} %bitcast.11, s32[8,256]{1,0:T(8,128)} %fusion.1.meta), custom_call_target="tpu_custom_call" | custom-call | tf_op jit(solution)/shard_map/curvature/pallas_call | solution.py:423
  171.7 1.4 reshape.11
  173.1 2.9 %copy.18 = bf16[1,192,5120]{2,1,0:T(8,128)(2,1)} copy(bf16[1,192,5120]{2,1,0:T(8,128)(2,1)} %bitcast.13) | data formatting | bytes 3932160
  (2 shorter events, 0.0 us)

commit v3 on v2

v3 whole, which is shorter than its diff:
```python
import functools
import math

import jax
import jax.numpy as jnp
from jax import lax
from jax.experimental import pallas as pl
from jax.experimental.pallas import tpu as pltpu
from jax.sharding import PartitionSpec as P

QUERY_HEADS = 40
KEY_VALUE_HEADS = 8
HEAD_SIZE = 128
TOK = 192
META = 16
CAP = 7
OWNERS = 32
RING = 4
GROUP = QUERY_HEADS // KEY_VALUE_HEADS
KV_LOCAL = KEY_VALUE_HEADS // RING
Q_COLS = QUERY_HEADS * HEAD_SIZE // RING
K_COLS = KV_LOCAL * HEAD_SIZE
SLOTS = 8 * RING
WINDOW = 4 * TOK
BEHIND = 3 * TOK
LINE = 8
CHUNKS = ((0, 0, 5), (1, 5, 5))
VMEM = 60 * 1024 * 1024
MESH = pl.DeviceIdType.MESH
F32 = jnp.float32
BF16 = jnp.bfloat16


def turned_dot(a, b):
    return lax.dot_general(a, b, (((0,), (0,)), ((), ())), preferred_element_type=F32)


def dot_t(a, b):
    return lax.dot_general(a, b, (((1,), (1,)), ((), ())), preferred_element_type=F32)


def one_hot(row, count):
    iota = lax.broadcasted_iota(jnp.int32, (count, row.shape[1]), 0).astype(F32)
    return jnp.where(iota == row, 1.0, 0.0).astype(BF16)


def kernel(token_total, q, kv, cot, meta, result, curve,
           qbuf, cbuf, kvbuf0, kvbuf1, qslots, cslots, kvslots, kvs, bias, slots, owned, acc, grads,
           parts, yparts, xparts, cparts,
           loc, kvsend, kvrecv, msend, mrecv, qsend, qrecv, csend, crecv, zsend, zrecv, ysend, yrecv, yfsend, yfrecv,
           yzsend, yzrecv, yzfsend, yzfrecv, osend, orecv, gsend, grecv, bsend, brecv, xsend, xrecv, psend, precv):
    kvbuf = (kvbuf0, kvbuf1)
    me = lax.axis_index("ctx")
    dp = lax.axis_index("dp")
    core = lax.rem(dp, 2)
    scale = 1.0 / math.sqrt(HEAD_SIZE)
    exponent = scale * math.log2(math.e)

    def turn(n):
        fast, slow = lax.rem(n, 4), n // 8
        return (slow + core * (fast - slow)) * 8 + lax.rem(n // 4, 2) * 4 + fast + core * (slow - fast)

    here = turn(me)
    x = lax.rem(here, RING)
    base = here - x
    zoff = lax.rem(here // 4, 2)
    y = here // 8
    zhere = here + 4 - 8 * zoff
    zbase = zhere - x
    line = zoff * 4 + dp // 2
    directions = (1, 3, 2)
    ways = (1, 3)

    def peer(place):
        return (dp, turn(place))

    def owner(t):
        return (dp, t)

    def line_peer(d):
        n = lax.rem(line + d, LINE)
        return (lax.rem(n, 4) * 2 + core, me + 4 * (n // 4 - zoff))

    core_peer = (dp + 1 - 2 * core, me)

    def up(d):
        return lax.rem(x + d, RING)

    def down(d):
        return lax.rem(x + RING - d, RING)

    def y_peer(d):
        return peer(lax.rem(here + 8 * d, OWNERS))

    def y_base(first, d):
        return lax.rem(first + OWNERS - 8 * d, OWNERS)

    def forward_way(i):
        return 1 if i < 2 else 3

    def send(src, dst, sems, at, device):
        return pltpu.make_async_remote_copy(
            src, dst, sems[0].at[at], sems[1].at[at], device_id=device, device_id_type=MESH)

    def kv_copy(a, d, half, to):
        return send(
            kv.at[:, pl.ds((half * RING + up(d)) * K_COLS + a * HEAD_SIZE, HEAD_SIZE)],
            kvbuf[a].at[to, pl.ds(0, TOK), pl.ds(half * HEAD_SIZE, HEAD_SIZE)],
            (kvsend, kvrecv), (a, d, half), peer(base + up(d)))

    def q_copy(c, d, to):
        _, first, count = CHUNKS[c]
        return send(
            q.at[:, pl.ds(up(d) * Q_COLS + first * HEAD_SIZE, count * HEAD_SIZE)],
            qbuf.at[to, :, pl.ds(first * HEAD_SIZE, count * HEAD_SIZE)], (qsend, qrecv), (c, d), peer(base + up(d)))

    def c_copy(c, d, to):
        _, first, count = CHUNKS[c]
        return send(
            cot.at[:, :, pl.ds(up(d) * Q_COLS + first * HEAD_SIZE, count * HEAD_SIZE)],
            cbuf.at[to, :, :, pl.ds(first * HEAD_SIZE, count * HEAD_SIZE)], (csend, crecv), (c, d), peer(base + up(d)))

    def meta_copy(d, to):
        return send(meta, kvbuf0.at[to, pl.ds(TOK, META)], (msend, mrecv), d, peer(base + up(d)))

    def z_copy(a, i, first):
        ref = kvbuf[a].at[first + i]
        return send(ref, ref, (zsend, zrecv), (a, i), peer(zhere))

    def y_copy(a, d, first):
        ref = kvbuf[a].at[pl.ds(first, RING)]
        return send(ref, ref, (ysend, yrecv), (a, d), y_peer(d))

    def y_forward(a, d, first):
        ref = kvbuf[a].at[pl.ds(first + (0 if d == 1 else 2), 2)]
        return send(ref, ref, (yfsend, yfrecv), (a, d), y_peer(d))

    def yz_copy(a, d, i, first):
        ref = kvbuf[a].at[first + i]
        return send(ref, ref, (yzsend, yzrecv), (a, d, i), y_peer(d))

    def yz_forward(a, i, first):
        ref = kvbuf[a].at[first + i]
        return send(ref, ref, (yzfsend, yzfrecv), (a, i), y_peer(forward_way(i)))

    def place_cols(c, place):
        _, first, count = CHUNKS[c]
        return pl.ds(pl.multiple_of(lax.rem(place, RING) * Q_COLS + first * HEAD_SIZE, 128), count * HEAD_SIZE)

    def chunk_cols(c):
        _, first, count = CHUNKS[c]
        return pl.ds(first * HEAD_SIZE, count * HEAD_SIZE)

    def o_copy(c, d, target, source):
        return send(
            slots.at[target, :, chunk_cols(c)], owned.at[source // RING, :, place_cols(c, source)],
            (osend, orecv), (c, d), owner(target))

    def o_local(c):
        return pltpu.make_async_copy(
            slots.at[me, :, chunk_cols(c)], owned.at[here // RING, :, place_cols(c, here)], loc.at[c, 2])

    def kv_local(a, half):
        return pltpu.make_async_copy(
            kv.at[:, pl.ds((half * RING + x) * K_COLS + a * HEAD_SIZE, HEAD_SIZE)],
            kvbuf[a].at[here, pl.ds(0, TOK), pl.ds(half * HEAD_SIZE, HEAD_SIZE)], loc.at[a, 3 + half])

    def q_local(c):
        _, first, count = CHUNKS[c]
        return pltpu.make_async_copy(
            q.at[:, pl.ds(x * Q_COLS + first * HEAD_SIZE, count * HEAD_SIZE)], qbuf.at[x, :, chunk_cols(c)], loc.at[c, 0])

    def c_local(c):
        _, first, count = CHUNKS[c]
        return pltpu.make_async_copy(
            cot.at[:, :, pl.ds(x * Q_COLS + first * HEAD_SIZE, count * HEAD_SIZE)],
            cbuf.at[x, :, :, chunk_cols(c)], loc.at[c, 1])

    meta_local = pltpu.make_async_copy(meta, kvbuf0.at[here, pl.ds(TOK, META)], loc.at[0, 5])

    def tables(place):
        return kvbuf0[place, TOK: TOK + META, :].astype(F32)

    barrier = pltpu.get_barrier_semaphore()

    @pl.loop(1, OWNERS)
    def _(d):
        pl.semaphore_signal(barrier, inc=1, device_id=owner(lax.rem(me + d, OWNERS)), device_id_type=MESH)

    @pl.loop(1, LINE)
    def _(d):
        pl.semaphore_signal(barrier, inc=1, device_id=line_peer(d), device_id_type=MESH)

    pl.semaphore_signal(barrier, inc=1, device_id=core_peer, device_id_type=MESH)

    meta_local.start()
    for a in range(KV_LOCAL):
        for half in range(2):
            kv_local(a, half).start()
    for c in range(len(CHUNKS)):
        q_local(c).start()
        c_local(c).start()
    acc[...] = jnp.zeros_like(acc)
    for a in range(KV_LOCAL):
        kvs[a, pl.ds(0, BEHIND), :] = jnp.zeros((BEHIND, 2 * HEAD_SIZE), BF16)
    pl.semaphore_wait(barrier, OWNERS - 1 + LINE - 1 + 1)

    for d in directions:
        for half in range(2):
            kv_copy(0, d, half, here).start()
        meta_copy(d, here).start()
    for d in directions:
        for half in range(2):
            kv_copy(1, d, half, here).start()

    def rows_of(place):
        return one_hot(tables(place)[2:3], TOK)

    def ring_rows(a, first):
        for i in range(2):
            halves = [
                turned_dot(rows_of(first + 2 * i + j), kvbuf[a][first + 2 * i + j, :TOK, :])
                .reshape(OWNERS, 8, 2 * HEAD_SIZE) for j in range(2)
            ]
            kvslots[a, :, pl.ds(pl.multiple_of(8 * first + 16 * i, 16), 16), :] = (
                jnp.concatenate(halves, axis=1).astype(BF16))

    def ring_into(c, buf, put):
        count = CHUNKS[c][2] * HEAD_SIZE

        for i in range(2):
            halves = [
                turned_dot(rows_of(base + 2 * i + j), buf(2 * i + j)).reshape(OWNERS, 8, count) for j in range(2)
            ]
            put[:, pl.ds(pl.multiple_of(16 * i, 16), 16), chunk_cols(c)] = jnp.concatenate(halves, axis=1).astype(BF16)

    def queries_in(c):
        ring_into(c, lambda s: qbuf[s, :, chunk_cols(c)], qslots)

    def cotangents_in(c):
        for p in range(2):
            ring_into(c, lambda s, p=p: cbuf[s, p, :, chunk_cols(c)], cslots.at[p])

    def wait_kv(a):
        for half in range(2):
            kv_local(a, half).wait()
        for d in directions:
            for half in range(2):
                kv_copy(a, d, half, base + down(d)).wait_recv()
            if a == 0:
                meta_copy(d, base + down(d)).wait_recv()
        if a == 0:
            meta_local.wait()

    def pass_z(a, pieces):
        for i in pieces:
            z_copy(a, i, zbase).wait_recv()
            for d in ways:
                yz_copy(a, d, i, zbase).start()

    def pass_y(a):
        for d in ways:
            y_copy(a, d, y_base(base, d)).wait_recv()
            y_forward(a, d, y_base(base, d)).start()

    def pass_yz(a):
        for i in range(RING):
            d = forward_way(i)
            yz_copy(a, d, i, y_base(zbase, d)).wait_recv()
            yz_forward(a, i, y_base(zbase, d)).start()

    slot_code = (lax.broadcasted_iota(jnp.int32, (SLOTS, TOK), 0) + base * 8).astype(F32)
    own_row = (lax.broadcasted_iota(jnp.int32, (SLOTS, TOK), 1) + BEHIND).astype(F32)
    key_at = lax.broadcasted_iota(jnp.int32, (SLOTS, WINDOW), 1).astype(F32)

    def mask(t):
        block = tables(turn(t))
        mine = slot_code == block[0:1, :TOK]
        row_at = jnp.sum(jnp.where(mine, own_row, 0.0), axis=1, keepdims=True)
        row_seg = jnp.sum(jnp.where(mine, block[1:2, :TOK], 0.0), axis=1, keepdims=True)
        key_seg = jnp.concatenate([block[:8], jnp.zeros((8, WINDOW - 256), F32)], axis=1)
        key_seg = pltpu.roll(key_seg, BEHIND, 1)
        for j in range(3):
            before = jnp.where(t + j >= 3, tables(turn(jnp.maximum(t + j - 3, 0)))[:8], 0.0)
            before = jnp.concatenate([before, jnp.zeros((8, WINDOW - 256), F32)], axis=1)
            key_seg += before if j == 0 else pltpu.roll(before, j * TOK, 1)
        allowed = (key_at <= row_at) & (key_seg[1:2] == row_seg)
        bias[t] = jnp.where(allowed, 0.0, -1e30)

    def last_keys(a):
        for i in range(RING):
            d = 4 - forward_way(i)
            yz_copy(a, d, i, y_base(zbase, d)).wait_recv()
        for d in ways:
            ring_rows(a, y_base(zbase, d))
        for d in ways:
            y_forward(a, d, y_base(base, 2)).wait_recv()
        ring_rows(a, y_base(base, 2))
        for i in range(RING):
            yz_forward(a, i, y_base(zbase, 2)).wait_recv()
        ring_rows(a, y_base(zbase, 2))

        @pl.loop(0, OWNERS // 4)
        def _(i):
            for j in range(4):
                t = 4 * i + j
                hot = one_hot(tables(turn(t))[0:1, :TOK], 256)
                kvs[a, pl.ds(pl.multiple_of(BEHIND + t * TOK, 64), TOK), :] = (
                    turned_dot(hot, kvslots[a, t]).astype(BF16))
                if a == 0:
                    mask(t)

    def wait_queries(c):
        q_local(c).wait()
        for d in directions:
            q_copy(c, d, down(d)).wait_recv()

    def wait_cotangents(c):
        c_local(c).wait()
        for d in directions:
            c_copy(c, d, down(d)).wait_recv()

    wait_kv(0)
    for i in range(RING):
        z_copy(0, i, base).start()
    for d in ways:
        y_copy(0, d, base).start()
    wait_kv(1)
    for i in range(RING):
        z_copy(1, i, base).start()

    for c in range(len(CHUNKS)):
        for d in directions:
            q_copy(c, d, x).start()
        for d in directions:
            c_copy(c, d, x).start()
    ring_rows(0, base)
    pass_z(0, (0, 1))
    pass_y(0)
    pass_z(0, (2, 3))
    for d in ways:
        y_copy(1, d, base).start()
    ring_rows(0, zbase)
    for d in ways:
        ring_rows(0, y_base(base, d))

    wait_queries(0)

    pass_yz(0)
    ring_rows(1, base)
    queries_in(0)
    pass_y(1)
    pass_z(1, range(RING))
    last_keys(0)

    wait_cotangents(0)
    cotangents_in(0)

    def attend(c, d, u):
        a, first, count = CHUNKS[c]
        t = lax.rem(me + d, OWNERS)
        start = pl.multiple_of(t * TOK, 64)

        def heads(ref):
            return jnp.concatenate(
                [ref[t, :, h * HEAD_SIZE: (h + 1) * HEAD_SIZE] for h in range(first, first + count)], axis=0)

        keys = kvs[a, pl.ds(start, WINDOW), :HEAD_SIZE]
        values = kvs[a, pl.ds(start, WINDOW), HEAD_SIZE:]
        scores = dot_t(heads(qslots), keys).reshape(count, SLOTS, WINDOW) + bias[t][None]
        top = jnp.max(scores, axis=2, keepdims=True)
        weights = jnp.exp2((scores - top) * exponent)
        probs = weights * (1.0 / jnp.sum(weights, axis=2, keepdims=True))
        mixed = jnp.dot(probs.astype(BF16).reshape(count * SLOTS, WINDOW), values, preferred_element_type=F32)
        for h in range(count):
            slots[t, :, (first + h) * HEAD_SIZE: (first + h + 1) * HEAD_SIZE] = (
                mixed[h * SLOTS: (h + 1) * SLOTS].astype(BF16))
        sums = []
        for p in range(2):
            upstream = heads(cslots.at[p])
            delta = jnp.sum(upstream.astype(F32) * mixed, axis=1, keepdims=True)
            grad = probs * (dot_t(upstream, values) - delta).reshape(count, SLOTS, WINDOW)
            sums.append(jnp.sum(grad.reshape(count, SLOTS // 8, 8, WINDOW), axis=1).reshape(count * 8, WINDOW))
        sums = jnp.concatenate(sums, axis=0)
        high = sums.astype(BF16)
        low = (sums - high.astype(F32)).astype(BF16)
        acc[c, u, : 4 * count * 8] += jnp.dot(jnp.concatenate([high, low], axis=0), keys, preferred_element_type=F32)

    def attend_some(c, begin, end):
        @pl.loop(begin, end)
        def _(i):
            for u in range(2):
                attend(c, 2 * i + u, u)

            @pl.when(i == 0)
            def _():
                o_local(c).start()

            @pl.when(i > 0)
            def _():
                o_copy(c, 2 * i, lax.rem(me + 2 * i, OWNERS), here).start()

            o_copy(c, 2 * i + 1, lax.rem(me + 2 * i + 1, OWNERS), here).start()

    attend_some(0, 0, OWNERS // 4)
    pass_yz(1)
    attend_some(0, OWNERS // 4, OWNERS // 2)

    ring_rows(1, zbase)
    for d in ways:
        ring_rows(1, y_base(base, d))
    last_keys(1)
    for c in (1,):
        wait_queries(c)
        queries_in(c)
        wait_cotangents(c)
        cotangents_in(c)
        attend_some(c, 0, OWNERS // 2)

    grads[...] = jnp.zeros_like(grads)
    for c, (_, first, count) in enumerate(CHUNKS):
        both = acc[c, 0] + acc[c, 1]
        step = count * 8
        for p in range(2):
            total = both[p * step: (p + 1) * step] + both[(2 + p) * step: (3 + p) * step]
            for h in range(count):
                row = jnp.sum(total[h * 8: (h + 1) * 8], axis=0, keepdims=True) * scale
                grads[pl.ds(p * 16 + first + h, 1), :] = row
    parts[pl.ds(line, 1)] = grads[...][None]

    def g_copy(d, at):
        return send(parts.at[at], parts.at[at], (gsend, grecv), d, line_peer(d))

    def b_copy(d, at):
        return send(yparts.at[at], yparts.at[at], (bsend, brecv), d, y_peer(d))

    def x_copy(d, at):
        return send(xparts.at[at], xparts.at[at], (xsend, xrecv), d, peer(base + up(d)))

    def p_copy(at):
        return send(cparts.at[at], cparts.at[at], (psend, precv), 0, core_peer)

    def into_rows(c):
        hot = one_hot(tables(here)[0:1, :TOK], 256)
        o_local(c).wait()

        @pl.loop(1, OWNERS)
        def _(d):
            o_copy(c, d, me, turn(lax.rem(me + OWNERS - d, OWNERS))).wait_recv()

        _, first, count = CHUNKS[c]
        for g in range(RING):
            cols = pl.ds(g * Q_COLS + first * HEAD_SIZE, count * HEAD_SIZE)
            result[:, cols] = turned_dot(hot, owned[:, :, cols].reshape(256, count * HEAD_SIZE)).astype(BF16)

    @pl.loop(1, LINE)
    def _(d):
        g_copy(d, line).start()


    @pl.loop(1, LINE)
    def _(d):
        g_copy(d, lax.rem(line + LINE - d, LINE)).wait_recv()
        g_copy(d, line).wait_send()

    yparts[pl.ds(y, 1)] = jnp.sum(parts[...], axis=0)[None]
    for d in directions:
        b_copy(d, y).start()
    for d in directions:
        b_copy(d, lax.rem(y + RING - d, RING)).wait_recv()
        b_copy(d, y).wait_send()
    xparts[pl.ds(x, 1)] = jnp.sum(yparts[...], axis=0)[None]
    for d in directions:
        x_copy(d, x).start()
    into_rows(0)
    for d in directions:
        x_copy(d, down(d)).wait_recv()
        x_copy(d, x).wait_send()
    cparts[pl.ds(core, 1)] = xparts[...][None]
    p_copy(core).start()
    p_copy(1 - core).wait_recv()
    p_copy(core).wait_send()
    total = cparts[0] + cparts[1]
    for g in range(RING):
        square = (total[g, :16] * total[g, :16] + total[g, 16:] * total[g, 16:]) / token_total
        heads_here = QUERY_HEADS // RING
        curve[g * heads_here: (g + 1) * heads_here, :] = square[:heads_here]
    into_rows(1)

    for d in directions:
        meta_copy(d, here).wait_send()

    @pl.loop(1, OWNERS)
    def _(d):
        for c in range(len(CHUNKS)):
            o_copy(c, d, lax.rem(me + d, OWNERS), here).wait_send()

    for c in range(len(CHUNKS)):
        for d in directions:
            q_copy(c, d, x).wait_send()
            c_copy(c, d, x).wait_send()
    for a in range(KV_LOCAL):
        for d in directions:
            for half in range(2):
                kv_copy(a, d, half, here).wait_send()
        for d in ways:
            y_copy(a, d, base).wait_send()
            y_forward(a, d, y_base(base, d)).wait_send()
            for i in range(RING):
                yz_copy(a, d, i, zbase).wait_send()
        for i in range(RING):
            z_copy(a, i, base).wait_send()
            yz_forward(a, i, y_base(zbase, forward_way(i))).wait_send()


def run(q, kv, cot, meta, token_total):
    hbm = pl.BlockSpec(memory_space=pl.ANY)
    vmem = pl.BlockSpec(memory_space=pltpu.VMEM)
    n = len(CHUNKS)

    def dma(*shape):
        return [pltpu.SemaphoreType.DMA(shape)] * 2

    return pl.pallas_call(
        functools.partial(kernel, token_total),
        out_shape=(
            jax.ShapeDtypeStruct((TOK, RING * Q_COLS), BF16),
            jax.ShapeDtypeStruct((QUERY_HEADS, HEAD_SIZE), F32),
        ),
        in_specs=[hbm] * 4,
        out_specs=(vmem, vmem),
        scratch_shapes=[
            pltpu.VMEM((RING, TOK, Q_COLS), BF16),
            pltpu.VMEM((RING, 2, TOK, Q_COLS), BF16),
            pltpu.VMEM((OWNERS, TOK + META, 2 * HEAD_SIZE), BF16),
            pltpu.VMEM((OWNERS, TOK, 2 * HEAD_SIZE), BF16),
            pltpu.VMEM((OWNERS, SLOTS, Q_COLS), BF16),
            pltpu.VMEM((2, OWNERS, SLOTS, Q_COLS), BF16),
            pltpu.VMEM((KV_LOCAL, OWNERS, 256, 2 * HEAD_SIZE), BF16),
            pltpu.VMEM((KV_LOCAL, BEHIND + OWNERS * TOK, 2 * HEAD_SIZE), BF16),
            pltpu.VMEM((OWNERS, SLOTS, WINDOW), F32),
            pltpu.VMEM((OWNERS, SLOTS, Q_COLS), BF16),
            pltpu.VMEM((OWNERS // RING, SLOTS, RING * Q_COLS), BF16),
            pltpu.VMEM((n, 2, 4 * GROUP * 8, HEAD_SIZE), F32),
            pltpu.VMEM((32, HEAD_SIZE), F32),
            pltpu.VMEM((LINE, 32, HEAD_SIZE), F32),
            pltpu.VMEM((RING, 32, HEAD_SIZE), F32),
            pltpu.VMEM((RING, 32, HEAD_SIZE), F32),
            pltpu.VMEM((2, RING, 32, HEAD_SIZE), F32),
            pltpu.SemaphoreType.DMA((n, 6)),
            *dma(KV_LOCAL, RING, 2), *dma(RING), *dma(n, RING), *dma(n, RING),
            *dma(KV_LOCAL, RING), *dma(KV_LOCAL, RING), *dma(KV_LOCAL, RING),
            *dma(KV_LOCAL, RING, RING), *dma(KV_LOCAL, RING), *dma(n, OWNERS),
            *dma(LINE), *dma(RING), *dma(RING), *dma(1),
        ],
        compiler_params=pltpu.CompilerParams(collective_id=0, has_side_effects=True, vmem_limit_bytes=VMEM),
        name="curvature",
    )(q, kv, cot, meta)


def per_device(queries, packed_keys_values, cotangents, send_rows, take_slots, segment_ids):
    sender = take_slots // CAP
    turned = (sender % 4) * 8 + (sender // 4 % 2) * 4 + sender // 8
    code = jnp.where(lax.axis_index("dp") % 2 == 0, sender, turned) * 8 + take_slots % CAP
    meta = jnp.concatenate([
        jnp.pad(code, ((0, 0), (0, 256 - TOK))),
        jnp.pad(segment_ids + 1, ((0, 0), (0, 256 - TOK))),
        jnp.pad(send_rows[0, 0], ((0, 0), (0, 8 - CAP)), constant_values=-1).reshape(1, 256),
        jnp.zeros((META - 3, 256), jnp.int32),
    ], axis=0).astype(BF16)
    cot = jnp.transpose(cotangents[0], (1, 0, 2))
    token_total = 2.0 * TOK * OWNERS * lax.axis_size("dp")
    out, curve = run(queries[0], packed_keys_values[0], cot, meta, token_total)
    return out[None], curve.reshape(-1)


def solution(mesh):
    placed = (
        P("dp", "ctx", None),
        P("dp", "ctx", None),
        P("dp", "ctx", None, None),
        P("dp", "ctx", None, None),
        P("dp", "ctx"),
        P("dp", "ctx"),
    )
    return jax.shard_map(
        per_device,
        mesh=mesh,
        in_specs=placed,
        out_specs=(P("dp", "ctx", None), P()),
        check_vma=False,
    )
```

time: 178 us -> 167 us (0.938)
  Pallas kernels: 164 us -> 155 us
    pallas_call x1, Pallas kernels: 164 us -> 155 us  [run(): pl.pallas_call(functools.partial(kernel, token_total), out_shape=(jax.Sha...]
    unnamed x3 -> x6, local copies, waits for them, and re-layouts: 8.66 us -> 8.61 us
where the time goes in v3:
time: 167 us; the launch traced here: 166 us
  Pallas kernels  155 us (93%)
  local copies, waits for them, and re-layouts  8.79 us (5%)
  other arithmetic  2.1 us (1%)
    pallas_call x1, Pallas kernels, run(): pl.pallas_call(functools.partial(kernel, token_total), out_shape=(jax.Sha...  155 us
    unnamed x6, local copies, waits for them, and re-layouts  8.61 us

profile of v3, /device:TPU:1, one launch (start us, length us, event | category | flops | bytes accessed | tf_op | source)
XLA Modules:
  0.0 166.5 jit_solution(3849795127802115902)
XLA Ops:
  0.7 0.1 pad.20.clone
  0.7 0.7 add_convert_fusion
  1.5 0.7 convert.21
  2.2 0.1 copy.14
  2.3 0.1 reshape.11
  2.4 0.7 fusion.5.meta
  3.0 4.9 %copy.16 = bf16[1,192,2,5120]{3,1,2,0:T(8,128)(2,1)} copy(bf16[1,192,2,5120]{3,2,1,0:T(2,128)(2,1)} %param.8) | data formatting | bytes 7864320 | tf_op args[2]
  8.0 154.9 %curvature.1 = (bf16[192,5120]{1,0:T(8,128)(2,1)}, f32[40,128]{1,0:T(8,128)}) custom-call(bf16[192,5120]{1,0:T(8,128)(2,1)} %bitcast.12, bf16[192,2048]{1,0:T(8,128)(2,1)} %bitcast.14, bf16[2,192,5120]{2,1,0:T(8,128)(2,1)} %bitcast.11, bf16[16,256]{1,0:T(8,128)(2,1)} %fusion.5.meta), custom_call_target="tpu_custom_call" | custom-call | tf_op jit(solution)/shard_map/curvature/pallas_call | solution.py:524
  162.9 0.0 copy-start
  162.9 2.9 %copy.19 = bf16[1,192,5120]{2,1,0:T(8,128)(2,1)} copy(bf16[1,192,5120]{2,1,0:T(8,128)(2,1)} %bitcast.13) | data formatting | bytes 3932160
  165.9 0.0 copy-done
  165.9 0.6 copy.20
  (2 shorter events, 0.0 us)
Async XLA Ops:
  162.9 3.0 %copy-start = (f32[40,128]{1,0:T(8,128)S(1)}, f32[40,128]{1,0:T(8,128)}, u32[]{:S(2)}) copy-start(f32[40,128]{1,0:T(8,128)} %get-tuple-element.5) | copy-start | bytes 61444

commit v4 on v3

--- a/solution.py
+++ b/solution.py
@@ -45,7 +45,7 @@
 
 
 def kernel(token_total, q, kv, cot, meta, result, curve,
-           qbuf, cbuf, kvbuf0, kvbuf1, qslots, cslots, kvslots, kvs, bias, slots, owned, acc, grads,
+           cotraw, cotp, qbuf, cbuf, kvbuf0, kvbuf1, qslots, cslots, kvslots, kvs, bias, slots, owned, acc, grads,
            parts, yparts, xparts, cparts,
            loc, kvsend, kvrecv, msend, mrecv, qsend, qrecv, csend, crecv, zsend, zrecv, ysend, yrecv, yfsend, yfrecv,
            yzsend, yzrecv, yzfsend, yzfrecv, osend, orecv, gsend, grecv, bsend, brecv, xsend, xrecv, psend, precv):
@@ -117,7 +117,7 @@
     def c_copy(c, d, to):
         _, first, count = CHUNKS[c]
         return send(
-            cot.at[:, :, pl.ds(up(d) * Q_COLS + first * HEAD_SIZE, count * HEAD_SIZE)],
+            cotp.at[:, :, pl.ds(up(d) * Q_COLS + first * HEAD_SIZE, count * HEAD_SIZE)],
             cbuf.at[to, :, :, pl.ds(first * HEAD_SIZE, count * HEAD_SIZE)], (csend, crecv), (c, d), peer(base + up(d)))
 
     def meta_copy(d, to):
@@ -173,10 +173,12 @@
     def c_local(c):
         _, first, count = CHUNKS[c]
         return pltpu.make_async_copy(
-            cot.at[:, :, pl.ds(x * Q_COLS + first * HEAD_SIZE, count * HEAD_SIZE)],
+            cotp.at[:, :, pl.ds(x * Q_COLS + first * HEAD_SIZE, count * HEAD_SIZE)],
             cbuf.at[x, :, :, chunk_cols(c)], loc.at[c, 1])
 
     meta_local = pltpu.make_async_copy(meta, kvbuf0.at[here, pl.ds(TOK, META)], loc.at[0, 5])
+
+    cot_local = pltpu.make_async_copy(cot, cotraw, loc.at[1, 5])
 
     def tables(place):
         return kvbuf0[place, TOK: TOK + META, :].astype(F32)
@@ -199,7 +201,7 @@
             kv_local(a, half).start()
     for c in range(len(CHUNKS)):
         q_local(c).start()
-        c_local(c).start()
+    cot_local.start()
     acc[...] = jnp.zeros_like(acc)
     for a in range(KV_LOCAL):
         kvs[a, pl.ds(0, BEHIND), :] = jnp.zeros((BEHIND, 2 * HEAD_SIZE), BF16)
@@ -329,11 +331,20 @@
     for i in range(RING):
         z_copy(1, i, base).start()
 
+    for d in directions:
+        q_copy(0, d, x).start()
+    cot_local.wait()
+
+    @pl.loop(0, TOK // 16)
+    def _(i):
+        rows = pl.ds(pl.multiple_of(16 * i, 16), 16)
+        for p in range(2):
+            cotp[p, rows, :] = cotraw[rows, p, :]
+
     for c in range(len(CHUNKS)):
-        for d in directions:
-            q_copy(c, d, x).start()
-        for d in directions:
-            c_copy(c, d, x).start()
+        c_local(c).start()
+    for d in directions:
+        c_copy(0, d, x).start()
     ring_rows(0, base)
     pass_z(0, (0, 1))
     pass_y(0)
@@ -345,6 +356,8 @@
         ring_rows(0, y_base(base, d))
 
     wait_queries(0)
+    for d in directions:
+        q_copy(1, d, x).start()
 
     pass_yz(0)
     ring_rows(1, base)
@@ -352,8 +365,13 @@
     pass_y(1)
     pass_z(1, range(RING))
     last_keys(0)
+    ring_rows(1, zbase)
+    for d in ways:
+        ring_rows(1, y_base(base, d))
 
     wait_cotangents(0)
+    for d in directions:
+        c_copy(1, d, x).start()
     cotangents_in(0)
 
     def attend(c, d, u):
@@ -406,9 +424,6 @@
     pass_yz(1)
     attend_some(0, OWNERS // 4, OWNERS // 2)
 
-    ring_rows(1, zbase)
-    for d in ways:
-        ring_rows(1, y_base(base, d))
     last_keys(1)
     for c in (1,):
         wait_queries(c)
@@ -530,6 +545,8 @@
         in_specs=[hbm] * 4,
         out_specs=(vmem, vmem),
         scratch_shapes=[
+            pltpu.VMEM((TOK, 2, RING * Q_COLS), BF16),
+            pltpu.VMEM((2, TOK, RING * Q_COLS), BF16),
             pltpu.VMEM((RING, TOK, Q_COLS), BF16),
             pltpu.VMEM((RING, 2, TOK, Q_COLS), BF16),
             pltpu.VMEM((OWNERS, TOK + META, 2 * HEAD_SIZE), BF16),
@@ -568,9 +585,8 @@
         jnp.pad(send_rows[0, 0], ((0, 0), (0, 8 - CAP)), constant_values=-1).reshape(1, 256),
         jnp.zeros((META - 3, 256), jnp.int32),
     ], axis=0).astype(BF16)
-    cot = jnp.transpose(cotangents[0], (1, 0, 2))
     token_total = 2.0 * TOK * OWNERS * lax.axis_size("dp")
-    out, curve = run(queries[0], packed_keys_values[0], cot, meta, token_total)
+    out, curve = run(queries[0], packed_keys_values[0], cotangents[0], meta, token_total)
     return out[None], curve.reshape(-1)
 
 

time: 167 us -> 156 us (0.934)
  Pallas kernels: 155 us -> 149 us
  local copies, waits for them, and re-layouts: 8.79 us -> 3.85 us
    pallas_call x1, Pallas kernels: 155 us -> 149 us  [run(): pl.pallas_call(functools.partial(kernel, token_total), out_shape=(jax.Sha...]
    unnamed x6 -> x5, local copies, waits for them, and re-layouts: 8.61 us -> 3.66 us
where the time goes in v4:
time: 156 us
  Pallas kernels  149 us (96%)
  local copies, waits for them, and re-layouts  3.85 us (2%)
  other arithmetic  2.1 us (1%)
    pallas_call x1, Pallas kernels, run(): pl.pallas_call(functools.partial(kernel, token_total), out_shape=(jax.Sha...  149 us
    unnamed x5, local copies, waits for them, and re-layouts  3.66 us

profile of v4, /device:TPU:1, one launch (start us, length us, event | category | flops | bytes accessed | tf_op | source)
XLA Modules:
  0.0 156.1 jit_solution(9654264976870318933)
XLA Ops:
  0.7 0.1 pad.20.clone
  0.7 0.7 add_convert_fusion
  1.5 0.7 convert.21
  2.2 0.1 copy.12
  2.3 0.1 reshape.11
  2.4 0.7 fusion.5.meta
  3.0 149.4 %curvature.1 = (bf16[192,5120]{1,0:T(8,128)(2,1)}, f32[40,128]{1,0:T(8,128)}) custom-call(bf16[192,5120]{1,0:T(8,128)(2,1)} %bitcast.8, bf16[192,2048]{1,0:T(8,128)(2,1)} %bitcast.10, bf16[192,2,5120]{2,1,0:T(2,128)(2,1)} %bitcast.7, bf16[16,256]{1,0:T(8,128)(2,1)} %fusion.5.meta), custom_call_target="tpu_custom_call" | custom-call | tf_op jit(solution)/shard_map/curvature/pallas_call | solution.py:539
  152.5 0.0 copy-start
  152.5 2.9 %copy.15 = bf16[1,192,5120]{2,1,0:T(8,128)(2,1)} copy(bf16[1,192,5120]{2,1,0:T(8,128)(2,1)} %bitcast.9) | data formatting | bytes 3932160
  155.4 0.0 copy-done
  155.4 0.6 copy.16
  (2 shorter events, 0.0 us)
Async XLA Ops:
  152.5 3.0 %copy-start = (f32[40,128]{1,0:T(8,128)S(1)}, f32[40,128]{1,0:T(8,128)}, u32[]{:S(2)}) copy-start(f32[40,128]{1,0:T(8,128)} %get-tuple-element.5) | copy-start | bytes 61444

commit v5 on v4

--- a/solution.py
+++ b/solution.py
@@ -356,8 +356,6 @@
         ring_rows(0, y_base(base, d))
 
     wait_queries(0)
-    for d in directions:
-        q_copy(1, d, x).start()
 
     pass_yz(0)
     ring_rows(1, base)
@@ -370,6 +368,8 @@
         ring_rows(1, y_base(base, d))
 
     wait_cotangents(0)
+    for d in directions:
+        q_copy(1, d, x).start()
     for d in directions:
         c_copy(1, d, x).start()
     cotangents_in(0)

time: 156 us -> 155 us (level)
  no operation moved by 1% of the time
where the time goes in v5:
time: 155 us
  Pallas kernels  148 us (95%)
  local copies, waits for them, and re-layouts  3.85 us (2%)
  other arithmetic  2.1 us (1%)
    pallas_call x1, Pallas kernels, run(): pl.pallas_call(functools.partial(kernel, token_total), out_shape=(jax.Sha...  148 us
    unnamed x5, local copies, waits for them, and re-layouts  3.66 us

profile of v5, /device:TPU:1, one launch (start us, length us, event | category | flops | bytes accessed | tf_op | source)
XLA Modules:
  0.0 155.1 jit_solution(17445021940236715972)
XLA Ops:
  0.7 0.1 pad.20.clone
  0.7 0.7 add_convert_fusion
  1.5 0.7 convert.21
  2.2 0.1 copy.12
  2.3 0.1 reshape.11
  2.4 0.7 fusion.5.meta
  3.0 148.5 %curvature.1 = (bf16[192,5120]{1,0:T(8,128)(2,1)}, f32[40,128]{1,0:T(8,128)}) custom-call(bf16[192,5120]{1,0:T(8,128)(2,1)} %bitcast.8, bf16[192,2048]{1,0:T(8,128)(2,1)} %bitcast.10, bf16[192,2,5120]{2,1,0:T(2,128)(2,1)} %bitcast.7, bf16[16,256]{1,0:T(8,128)(2,1)} %fusion.5.meta), custom_call_target="tpu_custom_call" | custom-call | tf_op jit(solution)/shard_map/curvature/pallas_call | solution.py:539
  151.5 0.0 copy-start
  151.5 2.9 %copy.15 = bf16[1,192,5120]{2,1,0:T(8,128)(2,1)} copy(bf16[1,192,5120]{2,1,0:T(8,128)(2,1)} %bitcast.9) | data formatting | bytes 3932160
  154.5 0.0 copy-done
  154.5 0.6 copy.16
  (2 shorter events, 0.0 us)
Async XLA Ops:
  151.5 3.0 %copy-start = (f32[40,128]{1,0:T(8,128)S(1)}, f32[40,128]{1,0:T(8,128)}, u32[]{:S(2)}) copy-start(f32[40,128]{1,0:T(8,128)} %get-tuple-element.5) | copy-start | bytes 61444
